TPU v7x, 32 devices: a whole 2x2x4 slice. The times are simulated.
32 devices in a mesh: grp: 2 (over x), fsdp: 4 (over z), item: 4 (over y, core).
Axes of the slice: x: 2, y: 2, z: 4, core: 2. Of those that a mesh axis runs over, the one named last changes fastest.
Arguments:
- hidden_states: bfloat16 [2048, 16, 4096], P(('grp', 'fsdp', 'item')), may hold values from -6 to 6
- positives: bfloat16 [2048, 1024], P(('grp', 'fsdp', 'item')), may hold values from -6 to 6
- negatives: int32 [2048, 32], P(('grp', 'fsdp', 'item')), may hold values from 0 to 4095, as said below
- lengths: int32 [2048], P(('grp', 'fsdp', 'item')), may hold values from 1 to 16, as said below
- norm_gain: bfloat16 [4096], replicated, may hold values from 0.25 to 1.75
- proj_weight: bfloat16 [4096, 1024], P('fsdp'), may hold values from -0.09375 to 0.09375
- pool_query: float32 [1024], replicated, may hold values from -6 to 6
- slab: bfloat16 [4096, 1024], P('item'), may hold values from -6 to 6
Outputs:
- grad_proj: float32 [4096, 1024], P('fsdp')
- grad_query: float32 [1024], replicated
- mean_loss: float32 [], replicated
Inputs may be any that keep to these rules, and one draw needn't show every extreme that they name: `negatives`: entries 8 o to 8 (o + 1) - 1 of each query's list are rows of owner block o, the slab rows 1024 o to 1024 (o + 1) - 1; a row may repeat. The first lengths[q] token slots of query q are valid.
All inputs are finite; a program needn't handle non-finite values.
Results may differ from a plain program's by a relative error of at most 0.0043.
Values may be sent and summed in bfloat16 or wider, within the bound.
No kernel may reach another device: no remote copies, remote signals or barrier semaphores. Data moves between devices by JAX's collectives and lax.ppermute only.
A program may use at most 128 MiB of HBM per device.

v0:
```python
import math

import jax
import jax.numpy as jnp
from jax import lax
from jax.sharding import PartitionSpec as P

sharpness_divisor = 0.05
norm_eps = 1e-05
embed_eps = 1e-06


def normalize(states, norm_gain):
    flat_states = states.reshape(-1, states.shape[-1]).astype(jnp.float32)
    inv_rms = lax.rsqrt(jnp.mean(flat_states * flat_states, axis=1, keepdims=True) + norm_eps)
    return (flat_states * inv_rms * norm_gain.astype(jnp.float32)).astype(jnp.bfloat16)


def gated_pool(token_proj, lengths, pool_query, seq_len):
    queries = lengths.shape[0]
    proj_width = token_proj.shape[1]
    tokens = token_proj.reshape(queries, seq_len, proj_width)
    gate_vals = jax.nn.sigmoid(
        jnp.einsum("qsp,p->qs", tokens, pool_query, precision=lax.Precision.HIGHEST)
        / math.sqrt(proj_width)
    )
    position = lax.broadcasted_iota(jnp.int32, (queries, seq_len), 1)
    weight = jnp.where(position < lengths[:, None], 1.0, 0.0).astype(jnp.float32) / lengths[
        :, None
    ].astype(jnp.float32)
    pooled = jnp.einsum("qs,qsp->qp", weight * gate_vals, tokens, precision=lax.Precision.HIGHEST)
    return (pooled, gate_vals, weight)


def unit_embed(pooled):
    proj_width = pooled.shape[1]
    unit_scale = lax.rsqrt(
        jnp.mean(pooled * pooled, axis=1, keepdims=True) + embed_eps
    ) / math.sqrt(proj_width)
    return ((pooled * unit_scale).astype(jnp.bfloat16), unit_scale)


def contrast(embedded, positives, neg_rows):
    proj_width = embedded.shape[1]
    matching_vector_fullprec = positives.astype(jnp.float32)
    matching_multiplier = lax.rsqrt(
        jnp.mean(matching_vector_fullprec * matching_vector_fullprec, axis=1) + embed_eps
    ) / math.sqrt(proj_width)
    matching_score = (
        jnp.einsum(
            "au,au->a",
            embedded.astype(jnp.float32),
            matching_vector_fullprec,
            precision=lax.Precision.HIGHEST,
        )
        * matching_multiplier
        / sharpness_divisor
    )
    row_sq = jnp.einsum("qnp,qnp->qn", neg_rows, neg_rows, preferred_element_type=jnp.float32)
    sample_multiplier = lax.rsqrt(row_sq / proj_width + embed_eps) / math.sqrt(proj_width)
    distractor_score = (
        jnp.einsum("ir,isr->is", embedded, neg_rows, preferred_element_type=jnp.float32)
        * sample_multiplier
        / sharpness_divisor
    )
    logits = jnp.concatenate([matching_score[:, None], distractor_score], axis=1)
    exp_logits = jnp.exp(logits)
    denom_sum = jnp.sum(exp_logits, axis=1, keepdims=True)
    prob = exp_logits / denom_sum
    loss_sum = jnp.sum(jnp.log(denom_sum[:, 0]) - matching_score)
    column = lax.broadcasted_iota(jnp.int32, logits.shape, 1)
    score_derivative = prob - jnp.where(column == 0, 1.0, 0.0).astype(jnp.float32)
    matching_contribution = (score_derivative[:, 0] * matching_multiplier / sharpness_divisor)[
        :, None
    ] * matching_vector_fullprec
    distractor_probability = (
        score_derivative[:, 1:] * sample_multiplier / sharpness_divisor
    ).astype(jnp.bfloat16)
    grad_embed = matching_contribution + jnp.einsum(
        "qn,qnp->qp", distractor_probability, neg_rows, preferred_element_type=jnp.float32
    )
    return (loss_sum, grad_embed)


def backward(token_proj, pooled, unit_scale, grad_embed, gate_vals, weight, pool_query, seq_len):
    queries, proj_width = pooled.shape
    tokens = token_proj.reshape(queries, seq_len, proj_width)
    mean_sq = jnp.mean(pooled * pooled, axis=1, keepdims=True)
    radial = jnp.sum(pooled * grad_embed, axis=1, keepdims=True)
    grad_pooled = unit_scale * grad_embed - pooled * radial * unit_scale / (
        proj_width * (mean_sq + embed_eps)
    )
    proj_dot = jnp.einsum("qsp,qp->qs", tokens, grad_pooled, precision=lax.Precision.HIGHEST)
    gate_slope = weight * gate_vals * (1.0 - gate_vals) * proj_dot / math.sqrt(proj_width)
    grad_tokens = (weight * gate_vals)[:, :, None] * grad_pooled[:, None, :] + gate_slope[
        :, :, None
    ] * pool_query[None, None, :]
    grad_query = jnp.einsum("qs,qsp->p", gate_slope, tokens, precision=lax.Precision.HIGHEST)
    return (grad_tokens.reshape(queries * seq_len, proj_width).astype(jnp.bfloat16), grad_query)


def body(hidden_states, positives, negatives, lengths, norm_gain, proj_weight, pool_query, slab):
    queries, seq_len, model_width = hidden_states.shape
    proj_width = proj_weight.shape[1]
    neg_count = negatives.shape[1]
    normed = normalize(hidden_states, norm_gain)

    def add_rows(shard_rows):
        return jnp.dot(normed, shard_rows, preferred_element_type=jnp.float32)

    def project():
        return add_rows(lax.all_gather(proj_weight, "fsdp", axis=0, tiled=True))

    token_proj = project()
    pooled, gate_vals, weight = gated_pool(token_proj, lengths, pool_query, seq_len)
    embedded, unit_scale = unit_embed(pooled)
    slab_piece = lax.all_gather(slab, "item", axis=0, tiled=True)
    inside = (negatives >= 0) & (negatives < slab_piece.shape[0])
    picked = jnp.take(slab_piece, jnp.clip(negatives, 0, slab_piece.shape[0] - 1), axis=0)
    neg_rows = jnp.where(
        inside[:, :, None], picked, jnp.zeros((queries, neg_count, proj_width), jnp.bfloat16)
    )
    loss_part, grad_embed = contrast(embedded, positives, neg_rows)
    token_proj = project()
    pooled, gate_vals, weight = gated_pool(token_proj, lengths, pool_query, seq_len)
    embedded, unit_scale = unit_embed(pooled)
    grad_tokens, query_part = backward(
        token_proj, pooled, unit_scale, grad_embed, gate_vals, weight, pool_query, seq_len
    )
    block_sum = lax.psum_scatter(
        lax.dot_general(
            normed, grad_tokens, (((0,), (0,)), ((), ())), preferred_element_type=jnp.float32
        ),
        ("fsdp", "item"),
        scatter_dimension=0,
        tiled=True,
    )
    block_sum = lax.psum(block_sum, "grp")
    grad_proj = lax.all_gather(block_sum, "item", axis=0, tiled=True)
    grad_query, loss_total = lax.psum((query_part, loss_part), ("grp", "fsdp", "item"))
    all_queries = queries * lax.axis_size("grp") * lax.axis_size("fsdp") * lax.axis_size("item")
    mean_loss = loss_total / all_queries
    return (grad_proj, grad_query, mean_loss)


def solution(mesh):
    return jax.shard_map(
        body,
        mesh=mesh,
        in_specs=(
            P(("grp", "fsdp", "item"), None, None),
            P(("grp", "fsdp", "item"), None),
            P(("grp", "fsdp", "item"), None),
            P(("grp", "fsdp", "item")),
            P(),
            P("fsdp", None),
            P(),
            P("item", None),
        ),
        out_specs=(P("fsdp", None), P(), P()),
        check_vma=False,
    )
```

profile of v0, /device:TPU:0, one launch (start us, length us, event | category | flops | bytes accessed | tf_op | source)
XLA Modules:
  0.0 545.8 jit_solution(15786612953614900187)
XLA Ops:
  7.2 0.0 copy-start.8
  7.2 0.0 copy-start.11
  7.2 0.0 copy-start.6
  7.2 0.0 all-gather.4.cloned.1.call-start
  7.2 0.7 all-gather.4.cloned.1.call-update
  7.9 0.0 all-gather.6.cloned.1.call-start
  8.0 0.7 all-gather.6.cloned.1.call-update
  8.7 0.0 reduce-scatter.2.cloned.1.call-start
  8.7 0.0 copy-done.8
  8.7 0.0 copy-done.11
  8.8 0.0 copy-done.6
  8.8 0.1 copy.14
  8.9 0.1 copy.15
  9.0 0.1 copy.16
  9.1 0.1 reshape.119
  9.2 5.1 fusion
  14.3 0.0 copy-start.7
  14.3 147.7 %all-gather.4.cloned.1.call-done = bf16[4096,1024]{1,0:T(8,128)(2,1)} async-done(((bf16[1024,1024]{1,0:T(8,128)(2,1)}), bf16[4096,1024]{1,0:T(8,128)(2,1)}) %all-gather.4.cloned.1.call-update) | async-done | bytes 8388624 | tf_op jit(solution)/shard_map/all_gather | solution.py:112
  162.0 12.9 %fusion.4 = f32[64,16,1024]{2,1,0:T(8,128)S(1)} fusion(bf16[4096,1024]{1,0:T(8,128)(2,1)} %all-gather.4.cloned.1.call-done, bf16[64,16,4096]{2,1,0:T(8,128)(2,1)} %param.8, f32[4096]{0:T(1024)S(1)} %convert_element_type.34, f32[64,16]{1,0:T(8,128)S(1)} %add_rsqrt_fusion), kind=kOutput, calls=%fused_computation.9 | convolution fusion | flops 8606711808 | bytes 20992000 | tf_op jit(solution)/shard_map/dot_general | solution.py:109
  174.9 0.0 copy-start
  174.9 2.0 copy-done
  176.9 0.0 copy-done.7
  176.9 14.7 %fusion.45 = f32[1,64,16]{2,0,1:T(1,128)S(1)} fusion(f32[64,16,1024]{2,1,0:T(8,128)S(1)} %fusion.4, f32[1024,1,1]{0,1,2:T(1,128)S(1)} %bitcast.90), kind=kOutput, calls=%fused_computation.79 | convolution fusion | flops 12582912 | bytes 4202496 | tf_op jit(solution)/shard_map/qsp,p->qs/dot_general | solution.py:24
  191.6 0.1 copy.18
  191.7 0.1 copy.19
  191.8 4.3 fusion.46
  196.1 0.1 fusion.18
  196.3 0.0 copy-done.3
  196.3 0.2 fusion.16
  196.5 0.0 copy-start.12
  196.5 23.6 %all-gather.6.cloned.1.call-done = bf16[4096,1024]{1,0:T(8,128)(2,1)} async-done(((bf16[1024,1024]{1,0:T(8,128)(2,1)}), bf16[4096,1024]{1,0:T(8,128)(2,1)}) %all-gather.6.cloned.1.call-update) | async-done | bytes 8388624 | tf_op jit(solution)/shard_map/all_gather | solution.py:117
  220.1 15.7 %gather_fusion = bf16[2048,1024]{1,0:T(8,128)(2,1)} fusion(bf16[4096,1024]{1,0:T(8,128)(2,1)} %all-gather.6.cloned.1.call-done, s32[2048]{0:T(1024)S(1)} %broadcast_clamp_fusion), kind=kCustom, calls=%fused_computation | custom fusion | bytes 8396800 | tf_op jit(solution)/shard_map/jit(_take)/gather | solution.py:119
  235.8 4.0 fusion.3
  239.8 0.0 copy-done.2
  239.8 1.9 fusion.9
  241.6 0.1 copy.26
  241.7 0.1 copy.30
  241.9 0.1 divide_subtract_fusion
  242.0 0.4 copy-done.9
  242.4 0.1 copy.31
  242.5 0.0 copy-start.1
  242.5 2.9 fusion.8
  245.4 0.3 fusion.20
  245.7 0.3 fusion.23
  246.1 4.8 fusion.24
  250.9 0.1 copy.34
  251.0 0.0 copy-start.4
  251.0 0.6 add_convert_fusion
  251.6 16.5 %convolution_bitcast_fusion = f32[4096,1024]{1,0:T(8,128)} fusion(bf16[64,16,4096]{2,1,0:T(8,128)(2,1)} %param.8, f32[4096]{0:T(1024)S(1)} %convert_element_type.34, f32[64,16]{1,0:T(8,128)S(1)} %add_rsqrt_fusion, bf16[64,16,1024]{2,0,1:T(8,128)(2,1)S(1)} %add_convert_fusion), kind=kOutput, calls=%fused_computation.6 | convolution fusion | flops 8606711808 | bytes 27283456 | tf_op jit(solution)/shard_map/dot_general | solution.py:131
  268.1 0.0 copy-start.15
  268.2 0.0 reduce-scatter.2.cloned.1.call-update
  268.2 0.0 all-reduce.3.cloned.1.call-start
  268.2 178.7 %reduce-scatter.2.cloned.1.call-done = f32[256,1024]{1,0:T(8,128)} async-done(((f32[4096,1024]{1,0:T(8,128)}), f32[256,1024]{1,0:T(8,128)}) %reduce-scatter.2.cloned.1.call-update) | async-done | bytes 1048592 | tf_op jit(solution)/shard_map/reduce_scatter | solution.py:130
  446.9 0.0 all-reduce.3.cloned.1.call-update
  446.9 0.0 all-gather.8.cloned.1.call-start
  447.0 41.2 %all-reduce.3.cloned.1.call-done = f32[256,1024]{1,0:T(8,128)} async-done(((f32[256,1024]{1,0:T(8,128)}), f32[256,1024]{1,0:T(8,128)}) %all-reduce.3.cloned.1.call-update) | async-done | bytes 1048592 | tf_op jit(solution)/shard_map/psum | solution.py:138
  488.1 0.0 all-gather.8.cloned.1.call-update
  488.2 0.1 copy.37
  488.2 0.0 copy-done.10
  488.3 0.6 subtract_reduce_fusion
  488.9 3.9 fusion.47
  492.8 39.8 %all-reduce = (f32[1024]{0:T(1024)}, f32[]{:T(128)}) all-reduce(f32[1024]{0:T(1024)S(1)} %bitcast.91, f32[]{:T(128)} %subtract_reduce_fusion), channel_id=1, replica_groups=mesh['grp'=2,'fsdp'=4,'item'=4] {'grp','fsdp','item'}, use_global_device_ids=true, to_apply=%region_7.8 | all-reduce | flops 1025 | bytes 8200 | tf_op jit(solution)/shard_map/psum | solution.py:140
  533.3 0.0 all-gather.8.cloned.1.call-done
  533.3 4.8 copy.61
  (30 shorter events, 0.3 us)
Async XLA Ops:
  7.2 1.6 copy-start.8
  7.2 1.6 copy-start.11
  7.2 1.6 copy-start.6
  7.2 154.8 %all-gather.4.cloned.1.call-start = ((), (), s32[]{:S(2)}) async-start(), calls=%async_computation.1 | async-start | bytes 10485760 | tf_op jit(solution)/shard_map/all_gather | solution.py:112
  7.9 212.1 %all-gather.6.cloned.1.call-start = ((), (), s32[]{:S(2)}) async-start(), calls=%async_computation.2 | async-start | bytes 10485760 | tf_op jit(solution)/shard_map/all_gather | solution.py:117
  8.7 438.2 %reduce-scatter.2.cloned.1.call-start = ((), (), s32[]{:S(2)}) async-start(), calls=%async_computation.3 | async-start | bytes 17825792 | tf_op jit(solution)/shard_map/reduce_scatter | solution.py:130
  14.3 162.6 %copy-start.7 = (f32[1024]{0:T(1024)S(1)}, f32[1024]{0:T(1024)}, u32[]{:S(2)}) copy-start(f32[1024]{0:T(1024)} %param.14) | copy-start | bytes 12292
  174.9 2.0 copy-start
  176.9 19.4 %copy-start.3 = (bf16[64,1024]{1,0:T(8,128)(2,1)S(1)}, bf16[64,1024]{1,0:T(8,128)(2,1)}, u32[]{:S(2)}) copy-start(bf16[64,1024]{1,0:T(8,128)(2,1)} %param.9) | copy-start | bytes 393220
  196.5 45.3 %copy-start.14 = (f32[64]{0:T(128)}, f32[64]{0:T(128)S(1)}, u32[]{:S(2)}) copy-start(f32[64]{0:T(128)S(1)} %get-tuple-element.4) | copy-start | bytes 772
  196.5 45.5 %copy-start.12 = (f32[64]{0:T(128)}, f32[64]{0:T(128)S(1)}, u32[]{:S(2)}) copy-start(f32[64]{0:T(128)S(1)} %get-tuple-element.3) | copy-start | bytes 772
  235.8 4.0 copy-start.2
  241.9 0.5 copy-start.9
  242.5 3.5 copy-start.1
  251.0 17.1 %copy-start.4 = (f32[64,16]{0,1:T(8,128)}, f32[64,16]{0,1:T(8,128)S(1)}, u32[]{:S(2)}) copy-start(f32[64,16]{0,1:T(8,128)S(1)} %fusion.32) | copy-start | bytes 12292
  268.1 220.0 %copy-start.5 = (f32[64,16]{0,1:T(8,128)S(1)}, f32[64,16]{0,1:T(8,128)}, u32[]{:S(2)}) copy-start(f32[64,16]{0,1:T(8,128)} %copy-done.4) | copy-start | bytes 12292
  268.1 220.1 %copy-start.10 = (f32[64]{0:T(128)S(1)}, f32[64]{0:T(128)}, u32[]{:S(2)}) copy-start(f32[64]{0:T(128)} %copy-done.9) | copy-start | bytes 772
  268.1 220.1 %copy-start.13 = (f32[64]{0:T(128)S(1)}, f32[64]{0:T(128)}, u32[]{:S(2)}) copy-start(f32[64]{0:T(128)} %copy-done.12) | copy-start | bytes 772
  268.1 220.1 %copy-start.15 = (f32[64]{0:T(128)S(1)}, f32[64]{0:T(128)}, u32[]{:S(2)}) copy-start(f32[64]{0:T(128)} %copy-done.14) | copy-start | bytes 772
  268.2 219.9 %all-reduce.3.cloned.1.call-start = ((), (), s32[]{:S(2)}) async-start(), calls=%async_computation.4 | async-start | bytes 2097152 | tf_op jit(solution)/shard_map/psum | solution.py:138
  446.9 86.4 %all-gather.8.cloned.1.call-start = ((), (), s32[]{:S(2)}) async-start(), calls=%async_computation.5 | async-start | bytes 5242880 | tf_op jit(solution)/shard_map/all_gather | solution.py:139
Sparse Core Ops, SparseCore 0:
  9.6 152.3 all-gather.3
  163.5 56.5 all-gather.5
  268.3 178.5 reduce-scatter.1
  449.0 39.0 all-reduce.2
  489.6 35.0 all-gather.7
where the time goes:
time: 546 us
  waiting for transfers between devices  393 us (72%)
  matrix products  62 us (11%)
  blocking collectives  39.8 us (7%)
  local copies, waits for them, and re-layouts  23.9 us (4%)
  between operations  15.9 us (3%)
  other arithmetic  11.5 us (2%)
    reduce_scatter x1, waiting for transfers between devices, body(): lax.psum_scatter(lax.dot_general(normed, grad_tokens, (((0,), (0,)), ((),...  179 us
    all_gather x1, waiting for transfers between devices, project(): return add_rows(lax.all_gather(proj_weight, 'fsdp', axis=0, tiled=True))  148 us
    psum x1, waiting for transfers between devices, body(): block_sum = lax.psum(block_sum, 'grp')  41.2 us
    psum x1, blocking collectives, body(): lax.psum((query_part, loss_part), ('grp', 'fsdp', 'item'))  39.8 us
    all_gather x1, waiting for transfers between devices, body(): slab_piece = lax.all_gather(slab, 'item', axis=0, tiled=True)  23.6 us
    dot_general x1, matrix products, body(): lax.dot_general(normed, grad_tokens, (((0,), (0,)), ((), ())), preferred_...  16.5 us
    gather x1, local copies, waits for them, and re-layouts, body(): jnp.take(slab_piece, jnp.clip(negatives, 0, slab_piece.shape[0] - 1), axi...  15.7 us
    dot_general x1, matrix products, gated_pool(): jnp.einsum('qsp,p->qs', tokens, pool_query, precision=lax.Precision.HIGHEST)  14.7 us
  transfers between devices with their start and end apart: 5, of which 4 were waited for; matrix products, arithmetic and copies ran while one was open for 8% of the time, Pallas kernels for 0%

commit v1 on v0

v1 whole, which is shorter than its diff:
```python
import math

import jax
import jax.numpy as jnp
from jax import lax
from jax.sharding import PartitionSpec as P

sharpness_divisor = 0.05
norm_eps = 1e-05
embed_eps = 1e-06

EVERY = ("fsdp", "grp", "item")
PLANE = ("grp", "item")
F32 = jnp.float32
BF16 = jnp.bfloat16


def split_bf16(values):
    high = values.astype(BF16)
    low = (values - high.astype(F32)).astype(BF16)
    return high, low


def exact_rows(left, right, dims):
    high, low = split_bf16(left)
    both = lax.dot_general(
        jnp.concatenate([high, low], axis=0), right, (dims, ((), ())), preferred_element_type=F32
    )
    rows = left.shape[0]
    return both[:rows] + both[rows:]


def gather_small(piece, axis):
    n = lax.axis_size(axis)
    me = lax.axis_index(axis)
    whole = jnp.zeros((n,) + piece.shape, piece.dtype)
    whole = lax.dynamic_update_index_in_dim(whole, piece, me, 0)
    for k in range(1, n):
        got = lax.ppermute(piece, axis, [(i, (i + k) % n) for i in range(n)])
        whole = lax.dynamic_update_index_in_dim(whole, got, lax.rem(me - k + n, n), 0)
    return whole


def body(hidden_states, positives, negatives, lengths, norm_gain, proj_weight, pool_query, slab):
    queries, seq, width = hidden_states.shape
    proj_width = proj_weight.shape[1]
    neg_count = negatives.shape[1]
    n_item = lax.axis_size("item")
    n_plane = lax.axis_size("grp") * n_item
    n_all = n_plane * lax.axis_size("fsdp")
    me_item = lax.axis_index("item")
    root = math.sqrt(proj_width)

    share = proj_weight.shape[0] // n_plane
    place = lax.axis_index("grp") * n_item + me_item
    weight_share = lax.dynamic_slice_in_dim(proj_weight, place * share, share, 0)
    weight = lax.all_gather(weight_share, EVERY, axis=0, tiled=True)

    block_u = jnp.sum(proj_weight.astype(F32) * pool_query[None, :], axis=1)
    u = gather_small(block_u, "fsdp").reshape(width)

    own = neg_count // n_item
    lists = lax.all_to_all(negatives.reshape(queries, n_item, own), "item", 1, 0, tiled=True)
    lists = lists.reshape(n_item * queries, own) - me_item * slab.shape[0]
    row_ids = lax.broadcasted_iota(jnp.int32, (1, slab.shape[0]), 1)
    counts = jnp.zeros((n_item * queries, slab.shape[0]), F32)
    for k in range(own):
        counts = counts + jnp.where(lists[:, k : k + 1] == row_ids, 1.0, 0.0)
    slab_f32 = slab.astype(F32)
    slab_scale = (
        lax.rsqrt(jnp.mean(slab_f32 * slab_f32, axis=1) + embed_eps) / root / sharpness_divisor
    )
    pos_f32 = positives.astype(F32)
    pos_scale = lax.rsqrt(jnp.mean(pos_f32 * pos_f32, axis=1) + embed_eps) / root / sharpness_divisor

    states = hidden_states.astype(F32)
    inv_rms = lax.rsqrt(jnp.mean(states * states, axis=2, keepdims=True) + norm_eps)
    normed = (states * inv_rms * norm_gain.astype(F32)).astype(BF16)
    normed_f32 = normed.astype(F32)
    gate = jax.nn.sigmoid(jnp.sum(normed_f32 * u, axis=2) / root)
    position = lax.broadcasted_iota(jnp.int32, (queries, seq), 1)
    valid = jnp.where(position < lengths[:, None], 1.0, 0.0).astype(F32) / lengths[:, None].astype(F32)
    gated = valid * gate
    pool_rows = jnp.sum(gated[:, :, None] * normed_f32, axis=1)

    rows_slice = lax.all_to_all(pool_rows.astype(BF16), EVERY, 1, 0, tiled=True)

    pooled = exact_rows(pool_rows, weight, ((1,), (0,)))
    mean_sq = jnp.mean(pooled * pooled, axis=1, keepdims=True)
    unit_scale = lax.rsqrt(mean_sq + embed_eps) / root
    embedded = (pooled * unit_scale).astype(BF16)

    all_embedded = gather_small(embedded, "item").reshape(n_item * queries, proj_width)
    score = (
        lax.dot_general(all_embedded, slab, (((1,), (1,)), ((), ())), preferred_element_type=F32)
        * slab_scale[None, :]
    )
    heavy = counts * jnp.exp(score)
    part_denom = jnp.sum(heavy, axis=1, keepdims=True)
    part_grad = jnp.dot((heavy * slab_scale[None, :]).astype(BF16), slab, preferred_element_type=F32)
    part = jnp.concatenate([part_grad, jnp.broadcast_to(part_denom, (n_item * queries, 128))], axis=1)
    part = part.reshape(n_item, queries, proj_width + 128)
    total = lax.dynamic_index_in_dim(part, me_item, 0, keepdims=False)
    for k in range(1, n_item):
        piece = lax.dynamic_index_in_dim(part, lax.rem(me_item + k, n_item), 0, keepdims=False)
        total = total + lax.ppermute(piece, "item", [(i, (i + k) % n_item) for i in range(n_item)])
    pos_score = jnp.sum(embedded.astype(F32) * pos_f32, axis=1) * pos_scale
    pos_exp = jnp.exp(pos_score)
    denom = total[:, proj_width] + pos_exp
    loss_part = jnp.sum(jnp.log(denom) - pos_score)
    grad_embed = (
        (total[:, :proj_width] / denom[:, None])
        + ((pos_exp / denom - 1.0) * pos_scale)[:, None] * pos_f32
    )

    radial = jnp.sum(pooled * grad_embed, axis=1, keepdims=True)
    grad_pooled = unit_scale * grad_embed - pooled * radial * unit_scale / (
        proj_width * (mean_sq + embed_eps)
    )
    all_grad = lax.all_gather(grad_pooled.astype(BF16), EVERY, axis=0, tiled=True)

    back = exact_rows(grad_pooled, weight, ((1,), (1,)))
    slope = gated * (1.0 - gate) * jnp.sum(normed_f32 * back[:, None, :], axis=2) / root
    slope_rows = jnp.sum(slope[:, :, None] * normed_f32, axis=(0, 1))
    slope_sum, loss_total = lax.psum((slope_rows, loss_part), EVERY)
    grad_query = exact_rows(slope_sum[None, :], weight, ((1,), (0,)))[0]

    my_slope = lax.dynamic_slice_in_dim(
        slope_sum, lax.axis_index("fsdp") * proj_weight.shape[0] + place * share, share, 0
    )
    grad_slice = lax.dot_general(
        rows_slice, all_grad, (((0,), (0,)), ((), ())), preferred_element_type=F32
    ) + my_slope[:, None] * pool_query[None, :]
    grad_proj = lax.all_gather(grad_slice.astype(BF16), PLANE, axis=0, tiled=True).astype(F32)
    return (grad_proj, grad_query, loss_total / (queries * n_all))


def solution(mesh):
    return jax.shard_map(
        body,
        mesh=mesh,
        in_specs=(
            P(("grp", "fsdp", "item"), None, None),
            P(("grp", "fsdp", "item"), None),
            P(("grp", "fsdp", "item"), None),
            P(("grp", "fsdp", "item")),
            P(),
            P("fsdp", None),
            P(),
            P("item", None),
        ),
        out_specs=(P("fsdp", None), P(), P()),
        check_vma=False,
    )
```

time: 546 us -> 253 us (0.46)
  waiting for transfers between devices: 393 us -> 77.8 us
  matrix products: 62 us -> 25.4 us
  other arithmetic: 11.5 us -> 46.2 us
  starting transfers between devices: 0.19 us -> 20.9 us
    reduce_scatter x1 -> x0, waiting for transfers between devices: 179 us -> none  [body(): lax.psum_scatter(lax.dot_general(normed, grad_tokens, (((0,), (0,)), ((),...]
    all_gather x3, waiting for transfers between devices: 171 us -> 66.2 us  [the longest x1 43.7 us: body(): weight = lax.all_gather(weight_share, EVERY, axis=0, tiled=True)]
    psum x1 -> x0, waiting for transfers between devices: 41.2 us -> none  [body(): block_sum = lax.psum(block_sum, 'grp')]
    dot_general x8 -> x6, matrix products: 62 us -> 25.4 us  [the longest x3 18.3 us: exact_rows(): lax.dot_general(jnp.concatenate([high, low], axis=0), right, (dims, ((),...]
    reduce_sum x6 -> x11, other arithmetic: 6.35 us -> 38.1 us  [the longest x1 9.87 us: body(): pool_rows = jnp.sum(gated[:, :, None] * normed_f32, axis=1)]
    gather x1 -> x0, local copies, waits for them, and re-layouts: 15.7 us -> none  [body(): jnp.take(slab_piece, jnp.clip(negatives, 0, slab_piece.shape[0] - 1), axi...]
    ppermute x0 -> x9, starting transfers between devices: none -> 13.2 us  [the longest x6 9.95 us: gather_small(): got = lax.ppermute(piece, axis, [(i, (i + k) % n) for i in range(n)])]
    ppermute x0 -> x9, waiting for transfers between devices: none -> 11.5 us  [the longest x3 9.11 us: body(): lax.ppermute(piece, 'item', [(i, (i + k) % n_item) for i in range(n_item)])]
  transfers between devices with their start and end apart: 5 -> 14, of which waited for: 4 -> 7; matrix products, arithmetic and copies ran while one was open for 8% -> 25% of each run, Pallas kernels for 0% -> 0%
where the time goes in v1:
time: 253 us; the launch traced here: 252 us
  waiting for transfers between devices  77.8 us (31%)
  other arithmetic  46.2 us (18%)
  blocking collectives  41.3 us (16%)
  matrix products  25.4 us (10%)
  local copies, waits for them, and re-layouts  24.8 us (10%)
  starting transfers between devices  20.9 us (8%)
  between operations  16 us (6%)
    all_gather x1, waiting for transfers between devices, body(): weight = lax.all_gather(weight_share, EVERY, axis=0, tiled=True)  43.7 us
    psum x1, blocking collectives, body(): slope_sum, loss_total = lax.psum((slope_rows, loss_part), EVERY)  41.3 us
    all_gather x1, waiting for transfers between devices, body(): lax.all_gather(grad_slice.astype(BF16), PLANE, axis=0, tiled=True)  22.6 us
    dot_general x3, matrix products, exact_rows(): lax.dot_general(jnp.concatenate([high, low], axis=0), right, (dims, ((),...  18.3 us
    ppermute x6, starting transfers between devices, gather_small(): got = lax.ppermute(piece, axis, [(i, (i + k) % n) for i in range(n)])  9.95 us
    reduce_sum x1, other arithmetic, body(): pool_rows = jnp.sum(gated[:, :, None] * normed_f32, axis=1)  9.87 us
    ppermute x3, waiting for transfers between devices, body(): lax.ppermute(piece, 'item', [(i, (i + k) % n_item) for i in range(n_item)])  9.11 us
    reduce_sum x1, other arithmetic, body(): gate = jax.nn.sigmoid(jnp.sum(normed_f32 * u, axis=2) / root)  6.36 us
  transfers between devices with their start and end apart: 14, of which 7 were waited for; matrix products, arithmetic and copies ran while one was open for 25% of the time, Pallas kernels for 0%

profile of v1, /device:TPU:0, one launch (start us, length us, event | category | flops | bytes accessed | tf_op | source)
XLA Modules:
  0.0 252.5 jit_solution(11444497814241702454)
XLA Ops:
  7.3 1.7 constant_dynamic-slice_fusion.1
  9.0 2.1 multiply_reduce_fusion.1
  11.1 3.1 %collective-permute-start = (f32[1024]{0:T(1024)S(1)}, f32[1024]{0:T(1024)S(1)}, u32[]{:S(2)}, u32[]{:S(2)}) collective-permute-start(f32[1024]{0:T(1024)S(1)} %multiply_reduce_fusion.1), channel_id=1, source_target_pairs={{0,4},{4,8},{8,12},{12,0},{1,5},{5,9},{9,13},{13,1},{2,6},{6,10},{... | collective-permute-start | bytes 12296 | tf_op jit(solution)/shard_map/ppermute | solution.py:39
  14.1 2.6 %collective-permute-start.1 = (f32[1024]{0:T(1024)S(1)}, f32[1024]{0:T(1024)S(1)}, u32[]{:S(2)}, u32[]{:S(2)}) collective-permute-start(f32[1024]{0:T(1024)S(1)} %multiply_reduce_fusion.1), channel_id=1, source_target_pairs={{0,8},{4,12},{8,0},{12,4},{1,9},{5,13},{9,1},{13,5},{2,10},{6,14},... | collective-permute-start | bytes 12296 | tf_op jit(solution)/shard_map/ppermute | solution.py:39
  16.7 1.3 collective-permute-start.2
  18.1 0.7 reshape.187
  18.8 3.2 %all-to-all-start.1 = ((s32[4,1,512]{2,1,0:T(1,128)}), s32[4,1,512]{2,1,0:T(1,128)S(1)}, u32[]{:S(2)}, u32[]{:S(2)}) async-start(s32[4,1,512]{2,1,0:T(1,128)} %reshape.187), calls=%async_computation.1 | async-start | bytes 16384 | tf_op jit(solution)/shard_map/all_to_all | solution.py:63
  22.0 2.1 multiply_reduce_fusion
  24.2 5.1 %fusion = f32[64,16]{1,0:T(8,128)S(1)} fusion(bf16[64,16,4096]{2,1,0:T(8,128)(2,1)} %param.8), kind=kLoop, calls=%fused_computation.6 | loop fusion | flops 12581888 | bytes 8392704 | tf_op jit(solution)/shard_map/reduce_sum | solution.py:77
  29.4 0.2 copy.62
  29.9 0.3 dynamic_update_slice.29
  30.2 6.4 %fusion.3 = f32[64,16]{1,0:T(8,128)S(1)} fusion(f32[4096]{0:T(1024)S(1)} %bitcast.96, f32[4096]{0:T(1024)S(1)} %convert_element_type.82, f32[64,16]{1,0:T(8,128)S(1)} %add_rsqrt_fusion, bf16[64,16,4096]{2,1,0:T(8,128)(2,1)} %param.8), kind=kLoop, calls=%fused_computation.9 | loop fusion | flops 29359104 | bytes 8429568 | tf_op jit(solution)/shard_map/reduce_sum | solution.py:80
  36.6 9.9 %fusion.4 = f32[64,4096]{1,0:T(8,128)S(1)} fusion(f32[64,16]{1,0:T(8,128)S(1)} %divide_multiply_fusion, f32[4096]{0:T(1024)S(1)} %convert_element_type.82, f32[64,16]{1,0:T(8,128)S(1)} %add_rsqrt_fusion, bf16[64,16,4096]{2,1,0:T(8,128)(2,1)} %param.8), kind=kLoop, calls=%fused_computation.10 | loop fusion | flops 29097984 | bytes 9461760 | tf_op jit(solution)/shard_map/reduce_sum | solution.py:84
  46.5 0.1 subtract_convert_fusion
  46.7 0.5 broadcast.266
  47.2 0.8 reduce
  48.1 43.7 %all-gather.4.cloned.1.call-done = bf16[4096,1024]{1,0:T(8,128)(2,1)} async-done(((bf16[128,1024]{1,0:T(8,128)(2,1)}), bf16[4096,1024]{1,0:T(8,128)(2,1)}) %all-gather.4.cloned.1.call-update) | async-done | bytes 8388624 | tf_op jit(solution)/shard_map/all_gather | solution.py:57
  91.8 7.0 %fusion.10 = f32[128,1024]{0,1:T(8,128)S(1)} fusion(bf16[4096,1024]{1,0:T(8,128)(2,1)} %all-gather.4.cloned.1.call-done, bf16[64,4096]{1,0:T(8,128)(2,1)S(1)} %get-tuple-element.14, bf16[64,4096]{1,0:T(8,128)(2,1)S(1)} %get-tuple-element.15), kind=kOutput, calls=%fused_computation.22 | convolution fusion | flops 1075838976 | bytes 9961472 | tf_op jit(solution)/shard_map/dot_general | solution.py:26
  98.8 0.2 multiply_reduce_fusion.3
  99.0 0.5 rsqrt_multiply_fusion.2
  99.5 0.9 fusion.17
  100.4 0.3 collective-permute-start.3
  100.6 1.5 collective-permute-start.4
  102.1 1.2 collective-permute-start.5
  103.3 0.6 fusion.38
  103.9 1.7 copy.54
  105.6 0.9 broadcast_in_dim.94
  106.5 1.6 constant_dynamic-update-slice_fusion.3
  108.1 0.4 collective-permute-done.3
  108.5 1.7 copy.55
  110.2 1.7 copy.56
  111.9 2.0 collective-permute-done.5
  113.9 1.7 copy.57
  115.6 1.6 constant_dynamic-update-slice_fusion.2
  117.2 1.6 constant_dynamic-update-slice_fusion.1
  118.8 1.6 constant_dynamic-update-slice_fusion
  120.3 2.8 %fusion.39 = (f32[256]{0:T(256)S(1)}, f32[256,1024]{1,0:T(8,128)S(1)}) fusion(f32[1024]{0:T(1024)S(1)} %rsqrt_multiply_fusion, bf16[256,1024]{1,0:T(8,128)(2,1)} %bitcast.21, bf16[1024,1024]{1,0:T(8,128)(2,1)S(1)} %copy-done.1, s32[256]{0:T(256)S(1)} %bitcast.104, s32[256]{0:T(256)S(1)} %bitcast.105, s32[256]{0:T(256)} %bitcast.106, s32[256]{0:T(256)} %bitcast.107, ...), kind=kOutput, calls=%fused_computation.100 | convolution fusion | flops 543686400 | bytes 3683328 | tf_op jit(solution)/shard_map/dot_general | solution.py:95
  123.1 0.7 fusion.19
  124.1 0.9 constant_dynamic-slice_fusion
  125.0 1.7 collective-permute-start.6
  126.7 1.5 collective-permute-start.7
  128.2 0.2 copy.65
  128.5 5.5 %collective-permute-done.6 = f32[64,1152]{1,0:T(8,128)} collective-permute-done((f32[64,1152]{1,0:T(8,128)S(1)}, f32[64,1152]{1,0:T(8,128)}, u32[]{:S(2)}, u32[]{:S(2)}) %collective-permute-start.6) | collective-permute-done | bytes 294944 | tf_op jit(solution)/shard_map/ppermute | solution.py:106
  134.0 1.2 copy.59
  135.2 1.7 collective-permute-done.7
  136.9 1.1 copy.60
  138.0 1.9 collective-permute-done.8
  139.9 1.1 copy.61
  140.9 1.3 fusion.15
  142.3 0.2 multiply_reduce_fusion.2
  142.5 0.2 subtract_convert_fusion.1
  142.7 0.8 copy.63
  143.5 0.9 copy_bitcast_fusion
  144.5 4.4 %all-to-all-start = ((bf16[64,32,128]{2,0,1:T(8,128)(2,1)}), bf16[64,32,128]{2,0,1:T(8,128)(2,1)S(1)}, u32[]{:S(2)}, u32[]{:S(2)}) async-start(bf16[64,32,128]{2,0,1:T(8,128)(2,1)} %copy_bitcast_fusion), calls=%async_computation | async-start | bytes 1048576 | tf_op jit(solution)/shard_map/all_to_all | solution.py:86
  148.9 6.7 %fusion.21 = f32[128,4096]{1,0:T(8,128)S(1)} fusion(bf16[4096,1024]{1,0:T(8,128)(2,1)} %all-gather.4.cloned.1.call-done, bf16[64,1024]{0,1:T(8,128)(2,1)S(1)} %get-tuple-element.9, bf16[64,1024]{0,1:T(8,128)(2,1)S(1)} %get-tuple-element.10), kind=kOutput, calls=%fused_computation.58 | convolution fusion | flops 1074266112 | bytes 10747904 | tf_op jit(solution)/shard_map/dot_general | solution.py:26
  155.8 6.1 %fusion.5 = f32[64,16]{1,0:T(8,128)S(1)} fusion(f32[64,4096]{1,0:T(8,128)S(1)} %slice_add_fusion, f32[4096]{0:T(1024)S(1)} %convert_element_type.82, f32[64,16]{1,0:T(8,128)S(1)} %add_rsqrt_fusion, bf16[64,16,4096]{2,1,0:T(8,128)(2,1)} %param.8), kind=kLoop, calls=%fused_computation.11 | loop fusion | flops 29359104 | bytes 9461760 | tf_op jit(solution)/shard_map/reduce_sum | solution.py:123
  162.0 0.6 fusion.33
  162.7 4.6 %fusion.6 = f32[4096]{0:T(1024)S(1)} fusion(f32[64,16]{1,0:T(8,128)S(1)} %multiply_multiply_fusion, f32[4096]{0:T(1024)S(1)} %convert_element_type.82, f32[64,16]{1,0:T(8,128)S(1)} %add_rsqrt_fusion, bf16[64,16,4096]{2,1,0:T(8,128)(2,1)S(1)} %bitcast.93), kind=kLoop, calls=%fused_computation.12 | loop fusion | flops 29356032 | bytes 8429568 | tf_op jit(solution)/shard_map/reduce_sum | solution.py:124
  167.3 41.3 %all-reduce = (f32[4096]{0:T(1024)S(1)}, f32[]{:T(128)}) all-reduce(f32[4096]{0:T(1024)S(1)} %fusion.6, f32[]{:T(128)} %fusion.33), channel_id=1, replica_groups=mesh['grp'=2,'fsdp'=4,'item'=4] {'fsdp','grp','item'}, use_global_device_ids=true, to_apply=%region_12.13 | all-reduce | flops 4097 | bytes 32776 | tf_op jit(solution)/shard_map/psum | solution.py:125
  208.6 3.6 %fusion.9 = bf16[128,1024]{1,0:T(8,128)(2,1)} fusion(bf16[2048,128]{1,0:T(8,128)(2,1)S(1)} %bitcast.95, bf16[2048,1024]{1,0:T(8,128)(2,1)} %all-gather.6.cloned.1.call-done, f32[1024]{0:T(1024)S(1)} %copy-done.3, f32[128]{0:T(128)S(1)} %dynamic_slice.24), kind=kOutput, calls=%fused_computation.19 | convolution fusion | flops 537264128 | bytes 4985344 | tf_op jit(solution)/shard_map/dot_general | solution.py:131
  213.0 4.6 %fusion.25 = f32[2,1024]{1,0:T(2,128)S(1)} fusion(bf16[4096,1024]{1,0:T(8,128)(2,1)} %all-gather.4.cloned.1.call-done, bf16[1,4096]{1,0:T(2,128)(2,1)S(1)} %convert_element_type.104, bf16[1,4096]{1,0:T(2,128)(2,1)S(1)} %convert_element_type.101), kind=kOutput, calls=%fused_computation.68 | convolution fusion | flops 16809984 | bytes 8413184 | tf_op jit(solution)/shard_map/dot_general | solution.py:26
  217.6 0.6 slice_add_fusion.2
  218.2 22.6 %all-gather.8.cloned.1.call-done = bf16[1024,1024]{1,0:T(8,128)(2,1)} async-done(((bf16[128,1024]{1,0:T(8,128)(2,1)}), bf16[1024,1024]{1,0:T(8,128)(2,1)}) %all-gather.8.cloned.1.call-update) | async-done | bytes 2097168 | tf_op jit(solution)/shard_map/all_gather | solution.py:134
  240.7 4.1 %convert_element_type.99 = f32[1024,1024]{1,0:T(8,128)} convert(bf16[1024,1024]{1,0:T(8,128)(2,1)} %all-gather.8.cloned.1.call-done) | non-fusion elementwise | flops 1048576 | bytes 6291456 | tf_op jit(solution)/shard_map/convert_element_type | solution.py:134
  (57 shorter events, 1.3 us)
Async XLA Ops:
  7.2 10.9 %copy-start = (s32[64,32]{0,1:T(8,128)S(1)}, s32[64,32]{0,1:T(8,128)}, u32[]{:S(2)}) copy-start(s32[64,32]{0,1:T(8,128)} %param.10) | copy-start | bytes 24580
  7.2 22.2 %copy-start.4 = (bf16[4096]{0:T(1024)(128)(2,1)S(1)}, bf16[4096]{0:T(1024)(128)(2,1)}, u32[]{:S(2)}) copy-start(bf16[4096]{0:T(1024)(128)(2,1)} %param.12) | copy-start | bytes 24580
  7.2 22.2 %copy-start.5 = (s32[64]{0:T(128)S(1)}, s32[64]{0:T(128)}, u32[]{:S(2)}) copy-start(s32[64]{0:T(128)} %param.11) | copy-start | bytes 772
  7.2 22.2 %copy-start.2 = (bf16[64,1024]{1,0:T(8,128)(2,1)S(1)}, bf16[64,1024]{1,0:T(8,128)(2,1)}, u32[]{:S(2)}) copy-start(bf16[64,1024]{1,0:T(8,128)(2,1)} %param.9) | copy-start | bytes 393220
  7.2 84.6 %all-gather.4.cloned.1.call-start = ((), (), s32[]{:S(2)}) async-start(), calls=%async_computation.2 | async-start | bytes 8650752 | tf_op jit(solution)/shard_map/all_gather | solution.py:57
  11.1 18.6 %collective-permute-start = (f32[1024]{0:T(1024)S(1)}, f32[1024]{0:T(1024)S(1)}, u32[]{:S(2)}, u32[]{:S(2)}) collective-permute-start(f32[1024]{0:T(1024)S(1)} %multiply_reduce_fusion.1), channel_id=1, source_target_pairs={{0,4},{4,8},{8,12},{12,0},{1,5},{5,9},{9,13},{13,1},{2,6},{6,10},{... | collective-permute-start | bytes 12296 | tf_op jit(solution)/shard_map/ppermute | solution.py:39
  14.1 15.6 %collective-permute-start.1 = (f32[1024]{0:T(1024)S(1)}, f32[1024]{0:T(1024)S(1)}, u32[]{:S(2)}, u32[]{:S(2)}) collective-permute-start(f32[1024]{0:T(1024)S(1)} %multiply_reduce_fusion.1), channel_id=1, source_target_pairs={{0,8},{4,12},{8,0},{12,4},{1,9},{5,13},{9,1},{13,5},{2,10},{6,14},... | collective-permute-start | bytes 12296 | tf_op jit(solution)/shard_map/ppermute | solution.py:39
  16.7 13.1 %collective-permute-start.2 = (f32[1024]{0:T(1024)S(1)}, f32[1024]{0:T(1024)S(1)}, u32[]{:S(2)}, u32[]{:S(2)}) collective-permute-start(f32[1024]{0:T(1024)S(1)} %multiply_reduce_fusion.1), channel_id=1, source_target_pairs={{0,12},{4,0},{8,4},{12,8},{1,13},{5,1},{9,5},{13,9},{2,14},{6,2},{... | collective-permute-start | bytes 12296 | tf_op jit(solution)/shard_map/ppermute | solution.py:39
  18.8 27.9 %all-to-all-start.1 = ((s32[4,1,512]{2,1,0:T(1,128)}), s32[4,1,512]{2,1,0:T(1,128)S(1)}, u32[]{:S(2)}, u32[]{:S(2)}) async-start(s32[4,1,512]{2,1,0:T(1,128)} %reshape.187), calls=%async_computation.1 | async-start | bytes 16384 | tf_op jit(solution)/shard_map/all_to_all | solution.py:63
  22.0 186.6 %all-gather.6.cloned.1.call-start = ((), (), s32[]{:S(2)}) async-start(), calls=%async_computation.3 | async-start | bytes 4325376 | tf_op jit(solution)/shard_map/all_gather | solution.py:120
  46.6 73.7 %copy-start.1 = (bf16[1024,1024]{1,0:T(8,128)(2,1)S(1)}, bf16[1024,1024]{1,0:T(8,128)(2,1)}, u32[]{:S(2)}) copy-start(bf16[1024,1024]{1,0:T(8,128)(2,1)} %param.15) | copy-start | bytes 6291460
  100.4 8.1 %collective-permute-start.3 = (bf16[64,1024]{0,1:T(8,128)(2,1)}, bf16[64,1024]{0,1:T(8,128)(2,1)}, u32[]{:S(2)}, u32[]{:S(2)}) collective-permute-start(bf16[64,1024]{0,1:T(8,128)(2,1)} %get-tuple-element.11), channel_id=1, source_target_pairs={{0,1},{1,2},{2,3},{3,0},{4,5},{5,6},{6,7},{7,4},{8,9},{9,10},{10,1... | collective-permute-start | bytes 393224 | tf_op jit(solution)/shard_map/ppermute | solution.py:39
  100.6 9.6 %collective-permute-start.4 = (bf16[64,1024]{0,1:T(8,128)(2,1)}, bf16[64,1024]{0,1:T(8,128)(2,1)}, u32[]{:S(2)}, u32[]{:S(2)}) collective-permute-start(bf16[64,1024]{0,1:T(8,128)(2,1)} %get-tuple-element.11), channel_id=1, source_target_pairs={{0,2},{1,3},{2,0},{3,1},{4,6},{5,7},{6,4},{7,5},{8,10},{9,11},{10,... | collective-permute-start | bytes 393224 | tf_op jit(solution)/shard_map/ppermute | solution.py:39
  102.1 11.8 %collective-permute-start.5 = (bf16[64,1024]{0,1:T(8,128)(2,1)}, bf16[64,1024]{0,1:T(8,128)(2,1)}, u32[]{:S(2)}, u32[]{:S(2)}) collective-permute-start(bf16[64,1024]{0,1:T(8,128)(2,1)} %get-tuple-element.11), channel_id=1, source_target_pairs={{0,3},{1,0},{2,1},{3,2},{4,7},{5,4},{6,5},{7,6},{8,11},{9,8},{10,9... | collective-permute-start | bytes 393224 | tf_op jit(solution)/shard_map/ppermute | solution.py:39
  123.1 19.3 %copy-start.6 = (f32[64]{0:T(128)S(1)}, f32[64]{0:T(128)}, u32[]{:S(2)}) copy-start(f32[64]{0:T(128)} %get-tuple-element.31) | copy-start | bytes 772
  125.0 9.0 %collective-permute-start.6 = (f32[64,1152]{1,0:T(8,128)S(1)}, f32[64,1152]{1,0:T(8,128)}, u32[]{:S(2)}, u32[]{:S(2)}) collective-permute-start(f32[64,1152]{1,0:T(8,128)S(1)} %get-tuple-element.19), channel_id=1, source_target_pairs={{0,1},{1,2},{2,3},{3,0},{4,5},{5,6},{6,7},{7,4},{8,9},{9,10},{10,1... | collective-permute-start | bytes 884744 | tf_op jit(solution)/shard_map/ppermute | solution.py:106
  126.7 10.2 %collective-permute-start.7 = (f32[64,1152]{1,0:T(8,128)}, f32[64,1152]{1,0:T(8,128)S(1)}, u32[]{:S(2)}, u32[]{:S(2)}) collective-permute-start(f32[64,1152]{1,0:T(8,128)} %get-tuple-element.18), channel_id=1, source_target_pairs={{0,2},{1,3},{2,0},{3,1},{4,6},{5,7},{6,4},{7,5},{8,10},{9,11},{10,... | collective-permute-start | bytes 884744 | tf_op jit(solution)/shard_map/ppermute | solution.py:106
  128.2 11.6 %collective-permute-start.8 = (f32[64,1152]{1,0:T(8,128)}, f32[64,1152]{1,0:T(8,128)S(1)}, u32[]{:S(2)}, u32[]{:S(2)}) collective-permute-start(f32[64,1152]{1,0:T(8,128)} %get-tuple-element.17), channel_id=1, source_target_pairs={{0,3},{1,0},{2,1},{3,2},{4,7},{5,4},{6,5},{7,6},{8,11},{9,8},{10,9... | collective-permute-start | bytes 884744 | tf_op jit(solution)/shard_map/ppermute | solution.py:106
  144.5 64.2 %all-to-all-start = ((bf16[64,32,128]{2,0,1:T(8,128)(2,1)}), bf16[64,32,128]{2,0,1:T(8,128)(2,1)S(1)}, u32[]{:S(2)}, u32[]{:S(2)}) async-start(bf16[64,32,128]{2,0,1:T(8,128)(2,1)} %copy_bitcast_fusion), calls=%async_computation | async-start | bytes 1048576 | tf_op jit(solution)/shard_map/all_to_all | solution.py:86
  148.9 91.9 %all-gather.8.cloned.1.call-start = ((), (), s32[]{:S(2)}) async-start(), calls=%async_computation.4 | async-start | bytes 2359296 | tf_op jit(solution)/shard_map/all_gather | solution.py:134
  148.9 13.7 %slice-start = ((s8[8388608]{0:T(1024)(128)(4,1)}), s8[4194304]{0:T(1024)(128)(4,1)S(1)}, s32[]{:S(2)}) async-start(s8[8388608]{0:T(1024)(128)(4,1)} %bitcast.92), calls=%async_computation.5 | async-start | bytes 8388608
  155.7 7.0 %slice-start.1 = ((s8[8388608]{0:T(1024)(128)(4,1)}), s8[4194304]{0:T(1024)(128)(4,1)S(1)}, s32[]{:S(2)}) async-start(s8[8388608]{0:T(1024)(128)(4,1)} %bitcast.92), calls=%async_computation.6 | async-start | bytes 8388608
  155.8 52.8 %copy-start.3 = (f32[1024]{0:T(1024)S(1)}, f32[1024]{0:T(1024)}, u32[]{:S(2)}) copy-start(f32[1024]{0:T(1024)} %param.14) | copy-start | bytes 12292
Sparse Core Ops, SparseCore 0:
  11.5 80.2 all-gather.3
  143.6 64.0 all-gather.5
  212.4 28.2 all-gather.7

commit v2 on v1

v2 whole, which is shorter than its diff:
```python
import functools
import math

import jax
import jax.numpy as jnp
from jax import lax
from jax.experimental import pallas as pl
from jax.experimental.pallas import tpu as pltpu
from jax.sharding import PartitionSpec as P

sharpness_divisor = 0.05
norm_eps = 1e-05
embed_eps = 1e-06

EVERY = ("fsdp", "grp", "item")
PLANE = ("grp", "item")
F32 = jnp.float32
BF16 = jnp.bfloat16
LANES = 128
MIB = 1024 * 1024
VMEM = pl.BlockSpec(memory_space=pltpu.VMEM)
SMEM = pl.BlockSpec(memory_space=pltpu.SMEM)


def shape(dims, dtype):
    return jax.ShapeDtypeStruct(dims, dtype)


def call(kernel, outs, ins, name, flops=0, scratch=(), smem=0):
    moved = sum(math.prod(a.shape) * a.dtype.itemsize for a in list(ins) + list(outs))
    return pl.pallas_call(
        kernel,
        out_shape=outs,
        in_specs=[SMEM] * smem + [VMEM] * (len(ins) - smem),
        out_specs=[VMEM] * len(outs),
        scratch_shapes=scratch,
        cost_estimate=pl.CostEstimate(flops=flops, bytes_accessed=moved, transcendentals=0),
        compiler_params=pltpu.CompilerParams(vmem_limit_bytes=44 * MIB),
        name=name,
    )(*ins)


def shift(values, axis, k):
    n = lax.axis_size(axis)
    return lax.ppermute(values, axis, [(i, (i + k) % n) for i in range(n)])


def split_bf16(values):
    high = values.astype(BF16)
    low = (values - high.astype(F32)).astype(BF16)
    return high, low


def nt(left, right):
    return lax.dot_general(left, right, (((1,), (1,)), ((), ())), preferred_element_type=F32)


def tn(left, right):
    return lax.dot_general(left, right, (((0,), (0,)), ((), ())), preferred_element_type=F32)


def gate_kernel(seq, root, blocks, z_ref, normed_ref, u_ref, len_ref, *rest):
    out_refs, gated_ref, curve_ref, rows_ref = rest[:blocks], rest[blocks], rest[blocks + 1], rest[-1]
    step = pl.program_id(0)
    tokens = normed_ref.shape[0]
    count = tokens // seq
    normed = normed_ref[...]
    logit = jnp.sum(normed.astype(F32) * u_ref[...], axis=1, keepdims=True) / root
    gate = 1.0 / (1.0 + jnp.exp(-logit))
    slot = lax.rem(lax.broadcasted_iota(jnp.int32, (tokens, 1), 0), seq)
    valid = jnp.where(slot < len_ref[...], 1.0, 0.0) / len_ref[...].astype(F32)
    gated = valid * gate
    gated_ref[...] = gated
    curve_ref[...] = gated * (1.0 - gate) / root
    owner = lax.broadcasted_iota(jnp.int32, (tokens, count), 0) // seq
    mine = owner == lax.broadcasted_iota(jnp.int32, (tokens, count), 1)
    high, low = split_bf16(jnp.where(mine, gated, 0.0))
    both = tn(jnp.concatenate([high, low], axis=1), normed)
    rows_ref[pl.ds(pl.multiple_of(step * count, count), count), :] = both[:count] + both[count:]

    @pl.when(step == pl.num_programs(0) - 1)
    def _():
        width = out_refs[0].shape[1]
        for k in range(blocks):
            at = lax.rem(z_ref[0] + k, blocks) * width
            out_refs[k][...] = rows_ref[:, pl.ds(pl.multiple_of(at, LANES), width)].astype(BF16)


def gate_rows(z, normed, u, token_lengths, seq, root, blocks):
    tokens, width = normed.shape
    queries = tokens // seq
    group = 8 if queries % 8 == 0 else queries
    step_tokens = group * seq
    outs = [shape((queries, width // blocks), BF16)] * blocks + [shape((tokens, 1), F32)] * 2
    column = pl.BlockSpec((step_tokens, 1), lambda i: (i, 0))
    return pl.pallas_call(
        functools.partial(gate_kernel, seq, root, blocks),
        grid=(queries // group,),
        out_shape=outs,
        in_specs=[
            SMEM,
            pl.BlockSpec((step_tokens, width), lambda i: (i, 0)),
            pl.BlockSpec((1, width), lambda i: (0, 0)),
            column,
        ],
        out_specs=[pl.BlockSpec((queries, width // blocks), lambda i: (0, 0))] * blocks + [column] * 2,
        scratch_shapes=[pltpu.VMEM((queries, width), F32)],
        cost_estimate=pl.CostEstimate(
            flops=4 * tokens * width, bytes_accessed=2 * tokens * width, transcendentals=0
        ),
        compiler_params=pltpu.CompilerParams(vmem_limit_bytes=44 * MIB),
        name="gate_rows",
    )(z, normed, u, token_lengths)


def block_kernel(n, back, *refs):
    pieces, weight_ref, outs = refs[:n], refs[n], refs[n + 1 : 2 * n + 1]
    rows = pieces[0].shape[0]
    stack = jnp.concatenate([p[...] for p in pieces], axis=0)
    if len(refs) > 2 * n + 1:
        refs[-1][...] = stack
    product = nt(stack, weight_ref[...]) if back else jnp.dot(
        stack, weight_ref[...], preferred_element_type=F32
    )
    for k in range(n):
        outs[k][...] = product[k * rows : (k + 1) * rows].astype(outs[k].dtype)


def block_product(pieces, weight, back, keep):
    n = len(pieces)
    rows, depth = pieces[0].shape
    width = weight.shape[0] if back else weight.shape[1]
    outs = [shape((rows, width), F32)] + [shape((rows, width), BF16)] * (n - 1)
    if keep:
        outs.append(shape((n * rows, depth), BF16))
    return call(
        functools.partial(block_kernel, n, back), outs, list(pieces) + [weight],
        "block_back" if back else "block_forward", flops=2 * n * rows * depth * width,
    )


def embed_kernel(root, *refs):
    parts, (pooled_ref, unit_ref, embedded_ref) = refs[:-3], refs[-3:]
    pooled = parts[0][...]
    for part in parts[1:]:
        pooled = pooled + part[...].astype(F32)
    unit = lax.rsqrt(jnp.mean(pooled * pooled, axis=1, keepdims=True) + embed_eps) / root
    pooled_ref[...] = pooled
    unit_ref[...] = unit
    embedded_ref[...] = (pooled * unit).astype(BF16)


def count_kernel(n, at_ref, lists_ref, counts_ref):
    queries = counts_ref.shape[0] // n
    ids = lax.broadcasted_iota(jnp.int32, (queries, counts_ref.shape[1]), 1)
    for k in range(n):
        at = pl.multiple_of(at_ref[k] * queries, queries)
        lists = lists_ref[pl.ds(at, queries), :] - at_ref[n]
        total = jnp.zeros(ids.shape, F32)
        for entry in range(lists.shape[1]):
            total = total + jnp.where(lists[:, entry : entry + 1] == ids, 1.0, 0.0)
        counts_ref[k * queries : (k + 1) * queries, :] = total


def contrast_kernel(n, *refs):
    pieces, (slab_ref, scale_ref, counts_ref), outs = refs[:n], refs[n : n + 3], refs[n + 3 :]
    queries, width = pieces[0].shape
    embedded = jnp.concatenate([p[...] for p in pieces], axis=0)
    slab = slab_ref[...]
    scale = scale_ref[...]
    heavy = counts_ref[...] * jnp.exp(nt(embedded, slab) * scale)
    denom = jnp.sum(heavy, axis=1, keepdims=True)
    grad = jnp.dot((heavy * scale).astype(BF16), slab, preferred_element_type=F32)
    high, low = split_bf16(denom)
    lane = lax.broadcasted_iota(jnp.int32, (queries, LANES), 1)
    for k in range(n):
        part = slice(k * queries, (k + 1) * queries)
        outs[k][:, :width] = grad[part].astype(outs[k].dtype)
        if k == 0:
            tail = jnp.where(lane == 0, denom[part], 0.0)
        else:
            tail = jnp.where(lane == 0, high[part].astype(F32), jnp.where(lane == 1, low[part].astype(F32), 0.0))
        outs[k][:, width:] = tail.astype(outs[k].dtype)


def grad_kernel(n, root, *refs):
    parts = refs[:n]
    pos_ref, pooled_ref, unit_ref, embedded_ref, grad_ref, columns_ref, loss_ref = refs[n:]
    queries, width = pos_ref.shape
    total = parts[0][:, :width]
    denom = jnp.sum(parts[0][:, width:], axis=1, keepdims=True)
    for part in parts[1:]:
        total = total + part[:, :width].astype(F32)
        denom = denom + jnp.sum(part[:, width:].astype(F32), axis=1, keepdims=True)
    positive = pos_ref[...].astype(F32)
    scale = (
        lax.rsqrt(jnp.mean(positive * positive, axis=1, keepdims=True) + embed_eps)
        / root
        / sharpness_divisor
    )
    score = jnp.sum(embedded_ref[...].astype(F32) * positive, axis=1, keepdims=True) * scale
    pos_exp = jnp.exp(score)
    denom = denom + pos_exp
    loss_ref[...] = jnp.broadcast_to(jnp.sum(jnp.log(denom) - score), loss_ref.shape)
    grad_embed = total / denom + (pos_exp / denom - 1.0) * scale * positive
    pooled, unit = pooled_ref[...], unit_ref[...]
    mean_sq = jnp.mean(pooled * pooled, axis=1, keepdims=True)
    radial = jnp.sum(pooled * grad_embed, axis=1, keepdims=True)
    grad = unit * grad_embed - pooled * (radial * unit / (width * (mean_sq + embed_eps)))
    grad = grad.astype(BF16)
    grad_ref[...] = grad
    places = width // columns_ref.shape[2]
    cols = columns_ref.shape[2]
    for j in range(columns_ref.shape[0]):
        at = (j % places) * cols
        columns_ref[j] = grad[:, at : at + cols]


def slope_kernel(seq, blocks, z_ref, normed_ref, curve_ref, loss_ref, *rest):
    backs, outs, all_ref, sum_ref = rest[:blocks], rest[blocks : 2 * blocks], rest[-2], rest[-1]
    step = pl.program_id(0)
    tokens, width = normed_ref.shape
    count = tokens // seq
    depth = width // blocks

    @pl.when(step == 0)
    def _():
        sum_ref[...] = jnp.zeros_like(sum_ref)
        for k in range(blocks):
            at = lax.rem(z_ref[0] + k, blocks) * depth
            all_ref[:, pl.ds(pl.multiple_of(at, LANES), depth)] = backs[k][...].astype(F32)

    back = all_ref[pl.ds(pl.multiple_of(step * count, count), count), :]
    normed = normed_ref[...].astype(F32).reshape(count, seq, width)
    dots = jnp.sum(normed * back[:, None, :], axis=2, keepdims=True)
    slope = curve_ref[...].reshape(count, seq, 1) * dots
    heavy = (slope * normed).reshape(tokens // 8, 8, width)
    sum_ref[...] += jnp.sum(heavy, axis=0)

    @pl.when(step == pl.num_programs(0) - 1)
    def _():
        all_ref[0:1, :] = jnp.sum(sum_ref[...], axis=0, keepdims=True)
        for k in range(blocks):
            at = lax.rem(z_ref[0] + k, blocks) * depth
            outs[k][:, :depth] = all_ref[0:1, pl.ds(pl.multiple_of(at, LANES), depth)]
            outs[k][:, depth:] = loss_ref[...]


def slope_rows(z, normed, curve, loss, backs, seq):
    tokens, width = normed.shape
    blocks = len(backs)
    queries = tokens // seq
    group = 8 if queries % 8 == 0 else queries
    step_tokens = group * seq
    whole = lambda dims: pl.BlockSpec(dims, lambda i: (0, 0))
    return pl.pallas_call(
        functools.partial(slope_kernel, seq, blocks),
        grid=(queries // group,),
        out_shape=[shape((1, width // blocks + LANES), F32)] * blocks,
        in_specs=[
            SMEM,
            pl.BlockSpec((step_tokens, width), lambda i: (i, 0)),
            pl.BlockSpec((step_tokens, 1), lambda i: (i, 0)),
            whole((1, LANES)),
        ]
        + [whole((queries, width // blocks))] * blocks,
        out_specs=[whole((1, width // blocks + LANES))] * blocks,
        scratch_shapes=[pltpu.VMEM((queries, width), F32), pltpu.VMEM((8, width), F32)],
        cost_estimate=pl.CostEstimate(
            flops=4 * tokens * width, bytes_accessed=2 * tokens * width, transcendentals=0
        ),
        compiler_params=pltpu.CompilerParams(vmem_limit_bytes=44 * MIB),
        name="slope_rows",
    )(z, normed, curve, loss, *backs)


def columns_kernel(n, order_ref, grads_ref, *refs):
    pieces, out_ref, sorted_ref = refs[:n], refs[n], refs[n + 1]
    chunk = grads_ref.shape[1]
    for j in range(sorted_ref.shape[0] // chunk):
        sorted_ref[j * chunk : (j + 1) * chunk, :] = grads_ref[order_ref[j]]
    rows = pieces[0].shape[0]
    total = tn(sorted_ref[0:rows, :], pieces[0][...])
    for k in range(1, n):
        total = total + tn(sorted_ref[k * rows : (k + 1) * rows, :], pieces[k][...])
    out_ref[...] = total.T.astype(BF16)


def finish_kernel(n, place_ref, slope_ref, pool_ref, *refs):
    pieces, out_ref = refs[:n], refs[n]
    cols = pieces[0].shape[1]
    slope = slope_ref[...]
    for k in range(n):
        at = pl.ds(pl.multiple_of(place_ref[k] * cols, LANES), cols)
        out_ref[:, at] = pieces[k][...].astype(F32) + slope * pool_ref[:, at]


def body(hidden_states, positives, negatives, lengths, norm_gain, proj_weight, pool_query, slab):
    queries, seq, width = hidden_states.shape
    depth, proj_width = proj_weight.shape
    n_z, n_g, n_i = lax.axis_size("fsdp"), lax.axis_size("grp"), lax.axis_size("item")
    n_c = 2 if n_i % 2 == 0 else 1
    n_h = n_i // n_c
    n_all = n_z * n_g * n_i
    z, g, i = lax.axis_index("fsdp"), lax.axis_index("grp"), lax.axis_index("item")
    h, c = i // n_c, lax.rem(i, n_c)
    root = math.sqrt(proj_width)
    z_arr = z.reshape(1).astype(jnp.int32)
    steps_z = range(1, n_z)
    steps_i = range(1, n_i)

    def plane_shift(values, dg, dh, dc):
        pairs = []
        for pg in range(n_g):
            for ph in range(n_h):
                for pc in range(n_c):
                    to = ((pg + dg) % n_g) * n_i + ((ph + dh) % n_h) * n_c + (pc + dc) % n_c
                    pairs.append((pg * n_i + ph * n_c + pc, to))
        return lax.ppermute(values, PLANE, pairs)

    def plane_gather(own):
        got = {}
        for dg in range(n_g):
            for dh in range(n_h):
                got[dg, dh, 0] = own if dg == dh == 0 else plane_shift(own, dg, dh, 0)
        for dg in range(n_g):
            for dh in range(n_h):
                for dc in range(1, n_c):
                    got[dg, dh, dc] = plane_shift(got[dg, dh, 0], 0, 0, dc)
        return got

    def source(dg, dh, dc):
        return (
            lax.rem(g - dg + n_g, n_g),
            lax.rem(h - dh + n_h, n_h) * n_c + lax.rem(c - dc + n_c, n_c),
        )

    block_u = jnp.sum(proj_weight.astype(F32) * pool_query[None, :], axis=1).reshape(1, depth)
    u_parts = [block_u] + [shift(block_u, "fsdp", k) for k in steps_z]
    u = jnp.zeros((1, width), F32)
    for k in range(n_z):
        u = lax.dynamic_update_slice(u, u_parts[k], (0, lax.rem(z - k + n_z, n_z) * depth))

    states = hidden_states.reshape(-1, width).astype(F32)
    inv_rms = lax.rsqrt(jnp.mean(states * states, axis=1, keepdims=True) + norm_eps)
    normed = (states * inv_rms * norm_gain.astype(F32)).astype(BF16)

    own = negatives.shape[1] // n_i
    lists = lax.all_to_all(negatives.reshape(queries, n_i, own), "item", 1, 0, tiled=True)
    lists = lists.reshape(n_i * queries, own)
    origin = jnp.stack([lax.rem(i - k + n_i, n_i) for k in range(n_i)] + [i * slab.shape[0]])
    counts = call(
        functools.partial(count_kernel, n_i),
        [shape((n_i * queries, slab.shape[0]), F32)], [origin.astype(jnp.int32), lists], "list_counts", smem=1,
    )[0]
    slab_f32 = slab.astype(F32)
    slab_scale = (
        lax.rsqrt(jnp.mean(slab_f32 * slab_f32, axis=1) + embed_eps) / root / sharpness_divisor
    ).reshape(1, -1)

    token_lengths = jnp.broadcast_to(lengths[:, None], (queries, seq)).reshape(-1, 1)
    *sends, gated, curve = gate_rows(z_arr, normed, u, token_lengths, seq, root, n_z)

    pieces = [sends[0]] + [shift(sends[k], "fsdp", k) for k in steps_z]
    *parts, held = block_product(pieces, proj_weight, False, True)
    parts = [parts[0]] + [shift(parts[k], "fsdp", -k) for k in steps_z]
    row = shape((queries, proj_width), F32)
    pooled, unit, embedded = call(
        functools.partial(embed_kernel, root),
        [row, shape((queries, 1), F32), shape(row.shape, BF16)], parts, "embed",
    )

    pieces = [embedded] + [shift(embedded, "item", k) for k in steps_i]
    wide = (queries, proj_width + LANES)
    parts = call(
        functools.partial(contrast_kernel, n_i),
        [shape(wide, F32)] + [shape(wide, BF16)] * (n_i - 1),
        pieces + [slab, slab_scale, counts], "contrast",
        flops=4 * n_i * queries * slab.shape[0] * proj_width,
    )
    parts = [parts[0]] + [shift(parts[k], "item", -k) for k in steps_i]
    n_plane = n_g * n_i
    cols = proj_width // n_plane
    grad, grad_columns, loss = call(
        functools.partial(grad_kernel, n_i, root),
        [shape(row.shape, BF16), shape((n_all, queries, cols), BF16), shape((1, LANES), F32)],
        parts + [positives, pooled, unit, embedded], "grad_pooled",
    )

    spread = plane_gather(held)
    all_columns = lax.all_to_all(grad_columns, EVERY, 0, 0, tiled=True)
    keys = sorted(spread, key=lambda key: (key[2], key[0], key[1]))
    order = []
    for key in keys:
        from_g, from_i = source(*key)
        for k in range(n_z):
            order.append((lax.rem(z - k + n_z, n_z) * n_g + from_g) * n_i + from_i)
    block_columns = call(
        functools.partial(columns_kernel, len(keys)),
        [shape((depth, cols), BF16)],
        [jnp.stack(order).astype(jnp.int32), all_columns] + [spread[key] for key in keys], "grad_columns",
        flops=2 * n_all * queries * depth * cols, scratch=[pltpu.VMEM((n_all * queries, cols), BF16)], smem=1,
    )[0]
    finished = plane_gather(block_columns)

    pieces = [grad] + [shift(grad, "fsdp", k) for k in steps_z]
    backs = block_product(pieces, proj_weight, True, False)
    backs = [backs[0]] + [shift(backs[k], "fsdp", -k) for k in steps_z]
    slopes = slope_rows(z_arr, normed, curve, loss, backs, seq)
    slope = slopes[0]
    for k in steps_z:
        slope = slope + shift(slopes[k], "fsdp", k)
    slope = slope + sum(shift(slope, "grp", k) for k in range(1, n_g))
    slope = slope + sum(shift(slope, "item", k) for k in steps_i)
    mean_loss = slope[0, depth] / (queries * n_all)
    slope = slope[:, :depth]
    high, low = split_bf16(slope)
    low = lax.reduce_precision(slope - lax.reduce_precision(slope, 8, 7), 8, 7).astype(BF16)
    query_part = jnp.dot(jnp.concatenate([high, low], axis=0), proj_weight, preferred_element_type=F32)
    query_part = jnp.sum(query_part, axis=0, keepdims=True)
    grad_query = query_part + sum(shift(query_part, "fsdp", k) for k in steps_z)

    places = []
    for key in keys:
        from_g, from_i = source(*key)
        places.append(from_g * n_i + from_i)
    grad_proj = call(
        functools.partial(finish_kernel, len(keys)), [shape((depth, proj_width), F32)],
        [jnp.stack(places).astype(jnp.int32), slope.reshape(depth, 1), pool_query.reshape(1, -1)]
        + [finished[key] for key in keys], "finish", smem=1,
    )[0]
    return (grad_proj, grad_query.reshape(proj_width), mean_loss)


def solution(mesh):
    return jax.shard_map(
        body,
        mesh=mesh,
        in_specs=(
            P(("grp", "fsdp", "item"), None, None),
            P(("grp", "fsdp", "item"), None),
            P(("grp", "fsdp", "item"), None),
            P(("grp", "fsdp", "item")),
            P(),
            P("fsdp", None),
            P(),
            P("item", None),
        ),
        out_specs=(P("fsdp", None), P(), P()),
        check_vma=False,
    )
```

time: 253 us -> 223 us (0.88)
  blocking collectives: 41.3 us -> 0 us
  starting transfers between devices: 20.9 us -> 59.5 us
  Pallas kernels: 0 us -> 30.4 us
  matrix products: 25.4 us -> 0.39 us
  other arithmetic: 46.2 us -> 22 us
  waiting for transfers between devices: 77.8 us -> 91.2 us
  between operations: 16 us -> 2.86 us
  local copies, waits for them, and re-layouts: 24.8 us -> 15.9 us
    ppermute x9 -> x45, waiting for transfers between devices: 11.5 us -> 91.2 us  [the longest x31 80.1 us: shift(): return lax.ppermute(values, axis, [(i, (i + k) % n) for i in range(n)])]
    all_gather x3 -> x0, waiting for transfers between devices: 66.2 us -> none  [the longest x1 43.7 us: body(): weight = lax.all_gather(weight_share, EVERY, axis=0, tiled=True)]
    psum x1 -> x0, blocking collectives: 41.3 us -> none  [body(): slope_sum, loss_total = lax.psum((slope_rows, loss_part), EVERY)]
    ppermute x9 -> x45, starting transfers between devices: 13.2 us -> 53.1 us  [the longest x31 44.7 us: shift(): return lax.ppermute(values, axis, [(i, (i + k) % n) for i in range(n)])]
    pallas_call x0 -> x10, Pallas kernels: none -> 30.4 us  [the longest x8 15.4 us: call(): pl.pallas_call(kernel, out_shape=outs, in_specs=[SMEM] * smem + [VMEM] *...]
    reduce_sum x10 -> x2, other arithmetic: 35.9 us -> 7.13 us  [the longest x1 5.05 us: body(): jnp.mean(states * states, axis=1, keepdims=True) + norm_eps]
    dot_general x6 -> x1, matrix products: 25.4 us -> 0.39 us  [body(): jnp.dot(jnp.concatenate([high, low], axis=0), proj_weight, preferred_elem...]
    unnamed x24 -> x37, local copies, waits for them, and re-layouts: 1.21 us -> 12.4 us
  transfers between devices with their start and end apart: 14 -> 47, of which waited for: 7 -> 22; matrix products, arithmetic and copies ran while one was open for 25% -> 12% of each run, Pallas kernels for 0% -> 10%
where the time goes in v2:
time: 223 us; the launch traced here: 222 us
  waiting for transfers between devices  91.2 us (41%)
  starting transfers between devices  59.5 us (27%)
  Pallas kernels  30.4 us (14%)
  other arithmetic  22 us (10%)
  local copies, waits for them, and re-layouts  15.9 us (7%)
  between operations  2.86 us (1%)
    ppermute x31, waiting for transfers between devices, shift(): return lax.ppermute(values, axis, [(i, (i + k) % n) for i in range(n)])  80.1 us
    ppermute x31, starting transfers between devices, shift(): return lax.ppermute(values, axis, [(i, (i + k) % n) for i in range(n)])  44.7 us
    pallas_call x8, Pallas kernels, call(): pl.pallas_call(kernel, out_shape=outs, in_specs=[SMEM] * smem + [VMEM] *...  15.4 us
    unnamed x37, local copies, waits for them, and re-layouts  12.4 us
    convert_element_type x2, other arithmetic, body(): normed = (states * inv_rms * norm_gain.astype(F32)).astype(BF16)  11.1 us
    ppermute x14, waiting for transfers between devices, plane_shift(): return lax.ppermute(values, PLANE, pairs)  11.1 us
    pallas_call x1, Pallas kernels, gate_rows(): pl.pallas_call(functools.partial(gate_kernel, seq, root, blocks), grid=(q...  9.76 us
    ppermute x14, starting transfers between devices, plane_shift(): return lax.ppermute(values, PLANE, pairs)  8.34 us
  transfers between devices with their start and end apart: 47, of which 22 were waited for; matrix products, arithmetic and copies ran while one was open for 12% of the time, Pallas kernels for 10%

profile of v2, /device:TPU:0, one launch (start us, length us, event | category | flops | bytes accessed | tf_op | source)
XLA Modules:
  0.0 222.1 jit_solution(6996627467843114089)
XLA Ops:
  0.6 2.1 multiply_reduce_fusion.2
  2.7 5.1 %collective-permute-start.2 = (f32[1,1024]{1,0:T(1,128)S(1)}, f32[1,1024]{1,0:T(1,128)S(1)}, u32[]{:S(2)}, u32[]{:S(2)}) collective-permute-start(f32[1,1024]{1,0:T(1,128)S(1)} %bitcast.79), channel_id=1, source_target_pairs={{0,12},{4,0},{8,4},{12,8},{1,13},{5,1},{9,5},{13,9},{2,14},{6,2},{... | collective-permute-start | bytes 12296 | tf_op jit(solution)/shard_map/ppermute | solution.py:45
  7.8 1.0 collective-permute-start
  9.5 3.8 %all-to-all-start = ((s32[4,1,512]{2,1,0:T(1,128)}), s32[4,1,512]{2,1,0:T(1,128)}, u32[]{:S(2)}, u32[]{:S(2)}) async-start(s32[4,1,512]{2,1,0:T(1,128)} %reshape.87), calls=%async_computation | async-start | bytes 16384 | tf_op jit(solution)/shard_map/all_to_all | solution.py:349
  14.1 5.1 %multiply_reduce_fusion = f32[64,16]{1,0:T(8,128)S(1)} fusion(bf16[64,16,4096]{2,1,0:T(8,128)(2,1)} %param.8), kind=kLoop, calls=%fused_computation.3 | loop fusion | flops 12581888 | bytes 8392704 | tf_op jit(solution)/shard_map/reduce_sum | solution.py:345
  19.3 10.4 %fusion.1.normed_ref = bf16[1024,4096]{1,0:T(8,128)(2,1)} fusion(f32[4096]{0:T(1024)S(1)} %convert_element_type.30, f32[1024]{0:T(1024)S(1)} %rsqrt.23, bf16[64,16,4096]{2,1,0:T(8,128)(2,1)} %param.8), kind=kLoop, calls=%fused_computation.2 | loop fusion | flops 16777216 | bytes 16797696 | tf_op jit(solution)/shard_map/convert_element_type | solution.py:346
  30.2 9.8 %gate_rows.1 = (bf16[64,1024]{1,0:T(8,128)(2,1)S(1)}, bf16[64,1024]{1,0:T(8,128)(2,1)S(1)}, bf16[64,1024]{1,0:T(8,128)(2,1)S(1)}, bf16[64,1024]{1,0:T(8,128)(2,1...) custom-call(s32[1]{0:T(128)} %bitcast.8.z_ref, bf16[1024,4096]{1,0:T(8,128)(2,1)} %fusion.1.normed_ref, ...), custom_call_target="tpu_custom_call" | custom-call | flops 16777216 | bytes 8388608 | tf_op jit(solution)/shard_map/gate_rows/pallas_call | solution.py:96
  40.0 2.5 %collective-permute-start.3 = (bf16[64,1024]{1,0:T(8,128)(2,1)S(1)}, bf16[64,1024]{1,0:T(8,128)(2,1)S(1)}, u32[]{:S(2)}, u32[]{:S(2)}) collective-permute-start(bf16[64,1024]{1,0:T(8,128)(2,1)S(1)} %get-tuple-element.33), channel_id=1, source_target_pairs={{0,4},{4,8},{8,12},{12,0},{1,5},{5,9},{9,13},{13,1},{2,6},{6,10},{... | collective-permute-start | bytes 393224 | tf_op jit(solution)/shard_map/ppermute | solution.py:45
  42.5 0.9 collective-permute-start.4
  43.4 1.5 collective-permute-start.5
  45.3 2.9 %collective-permute-done.3.refs_1_ = bf16[64,1024]{1,0:T(8,128)(2,1)S(1)} collective-permute-done((bf16[64,1024]{1,0:T(8,128)(2,1)S(1)}, bf16[64,1024]{1,0:T(8,128)(2,1)S(1)}, u32[]{:S(2)}, u32[]{:S(2)}) %collective-permute-start.3) | collective-permute-done | bytes 131104 | tf_op jit(solution)/shard_map/ppermute | solution.py:45
  48.2 5.1 %collective-permute-done.4.refs_2_ = bf16[64,1024]{1,0:T(8,128)(2,1)S(1)} collective-permute-done((bf16[64,1024]{1,0:T(8,128)(2,1)S(1)}, bf16[64,1024]{1,0:T(8,128)(2,1)S(1)}, u32[]{:S(2)}, u32[]{:S(2)}) %collective-permute-start.4) | collective-permute-done | bytes 131104 | tf_op jit(solution)/shard_map/ppermute | solution.py:45
  53.4 1.4 block_forward.1
  54.8 4.0 %collective-permute-start.6 = (bf16[64,1024]{1,0:T(8,128)(2,1)}, bf16[64,1024]{1,0:T(8,128)(2,1)S(1)}, u32[]{:S(2)}, u32[]{:S(2)}) collective-permute-start(bf16[64,1024]{1,0:T(8,128)(2,1)} %get-tuple-element.37), channel_id=1, source_target_pairs={{0,12},{4,0},{8,4},{12,8},{1,13},{5,1},{9,5},{13,9},{2,14},{6,2},{... | collective-permute-start | bytes 393224 | tf_op jit(solution)/shard_map/ppermute | solution.py:45
  58.8 0.7 collective-permute-start.7
  61.3 2.0 reduce.1
  63.3 1.4 reshape.88
  64.6 6.9 %collective-permute-done.7.refs_2_ = bf16[64,1024]{1,0:T(8,128)(2,1)S(1)} collective-permute-done((bf16[64,1024]{1,0:T(8,128)(2,1)}, bf16[64,1024]{1,0:T(8,128)(2,1)S(1)}, u32[]{:S(2)}, u32[]{:S(2)}) %collective-permute-start.7) | collective-permute-done | bytes 131104 | tf_op jit(solution)/shard_map/ppermute | solution.py:45
  72.2 0.9 copy-done.10
  73.1 0.8 embed.1
  75.0 1.2 collective-permute-start.10
  76.4 0.7 bitcast_bitcast_fusion
  77.9 1.7 list_counts.1.refs_6_
  79.6 3.9 %collective-permute-done.10.refs_2_ = bf16[64,1024]{1,0:T(8,128)(2,1)S(1)} collective-permute-done((bf16[64,1024]{1,0:T(8,128)(2,1)}, bf16[64,1024]{1,0:T(8,128)(2,1)S(1)}, u32[]{:S(2)}, u32[]{:S(2)}) %collective-permute-start.10) | collective-permute-done | bytes 131104 | tf_op jit(solution)/shard_map/ppermute | solution.py:45
  83.5 1.6 copy-done.4
  85.8 2.3 %contrast.1 = (f32[64,1152]{1,0:T(8,128)S(1)}, bf16[64,1152]{1,0:T(8,128)(2,1)S(1)}, bf16[64,1152]{1,0:T(8,128)(2,1)S(1)}, bf16[64,1152]{1,0:T(8,128)(2,1)S(1)}) custom-call(bf16[64,1024]{1,0:T(8,128)(2,1)} %get-tuple-element.40.refs_0_.refs_7_, bf16[64,1024]{1,0:T(8,128)(2,1)} %collective-permute-done.9.refs_1_, ...), custom_call_target="tpu_custom_call" | custom-call | flops 1073741824 | bytes 4411392 | tf_op jit(solution)/shard_map/contrast/pallas_call | solution.py:31
  88.1 1.0 collective-permute-start.13
  89.3 2.0 collective-permute-start.30
  91.9 0.9 collective-permute-start.28
  92.8 14.8 %collective-permute-done.13.refs_2_ = bf16[64,1152]{1,0:T(8,128)(2,1)S(1)} collective-permute-done((bf16[64,1152]{1,0:T(8,128)(2,1)S(1)}, bf16[64,1152]{1,0:T(8,128)(2,1)S(1)}, u32[]{:S(2)}, u32[]{:S(2)}) %collective-permute-start.13) | collective-permute-done | bytes 147488 | tf_op jit(solution)/shard_map/ppermute | solution.py:45
  107.6 1.1 collective-permute-done.14.refs_3_
  108.8 1.3 grad_pooled.1
  110.1 0.8 copy-done.7
  110.9 2.6 %all-to-all-start.1 = ((bf16[32,64,128]{2,1,0:T(8,128)(2,1)}), bf16[32,64,128]{2,1,0:T(8,128)(2,1)S(1)}, u32[]{:S(2)}, u32[]{:S(2)}) async-start(bf16[32,64,128]{2,1,0:T(8,128)(2,1)} %copy-done.7), calls=%async_computation.1 | async-start | bytes 1048576 | tf_op jit(solution)/shard_map/all_to_all | solution.py:391
  113.6 3.7 %collective-permute-start.17 = (bf16[64,1024]{1,0:T(8,128)(2,1)S(1)}, bf16[64,1024]{1,0:T(8,128)(2,1)S(1)}, u32[]{:S(2)}, u32[]{:S(2)}) collective-permute-start(bf16[64,1024]{1,0:T(8,128)(2,1)S(1)} %get-tuple-element.48.refs_0_), channel_id=1, source_target_pairs={{0,12},{4,0},{8,4},{12,8},{1,13},{5,1},{9,5},{13,9},{2,14},{6,2},{... | collective-permute-start | bytes 393224 | tf_op jit(solution)/shard_map/ppermute | solution.py:45
  117.2 9.3 %collective-permute-done.17.refs_3_ = bf16[64,1024]{1,0:T(8,128)(2,1)S(1)} collective-permute-done((bf16[64,1024]{1,0:T(8,128)(2,1)S(1)}, bf16[64,1024]{1,0:T(8,128)(2,1)S(1)}, u32[]{:S(2)}, u32[]{:S(2)}) %collective-permute-start.17) | collective-permute-done | bytes 131104 | tf_op jit(solution)/shard_map/ppermute | solution.py:45
  126.5 11.5 %collective-permute-start.15 = (bf16[64,1024]{1,0:T(8,128)(2,1)S(1)}, bf16[64,1024]{1,0:T(8,128)(2,1)S(1)}, u32[]{:S(2)}, u32[]{:S(2)}) collective-permute-start(bf16[64,1024]{1,0:T(8,128)(2,1)S(1)} %get-tuple-element.48.refs_0_), channel_id=1, source_target_pairs={{0,4},{4,8},{8,12},{12,0},{1,5},{5,9},{9,13},{13,1},{2,6},{6,10},{... | collective-permute-start | bytes 393224 | tf_op jit(solution)/shard_map/ppermute | solution.py:45
  138.0 1.8 collective-permute-done.16.refs_2_
  139.8 0.7 collective-permute-done.15.refs_1_
  140.5 0.7 block_back.1
  141.3 0.9 collective-permute-start.18
  142.2 3.0 %collective-permute-start.19 = (bf16[64,1024]{1,0:T(8,128)(2,1)S(1)}, bf16[64,1024]{1,0:T(8,128)(2,1)S(1)}, u32[]{:S(2)}, u32[]{:S(2)}) collective-permute-start(bf16[64,1024]{1,0:T(8,128)(2,1)S(1)} %get-tuple-element.51), channel_id=1, source_target_pairs={{0,8},{4,12},{8,0},{12,4},{1,9},{5,13},{9,1},{13,5},{2,10},{6,14},... | collective-permute-start | bytes 393224 | tf_op jit(solution)/shard_map/ppermute | solution.py:45
  145.8 0.9 collective-permute-done.18.rest_1_
  146.7 8.3 %collective-permute-done.19.rest_2_ = bf16[64,1024]{1,0:T(8,128)(2,1)S(1)} collective-permute-done((bf16[64,1024]{1,0:T(8,128)(2,1)S(1)}, bf16[64,1024]{1,0:T(8,128)(2,1)S(1)}, u32[]{:S(2)}, u32[]{:S(2)}) %collective-permute-start.19) | collective-permute-done | bytes 131104 | tf_op jit(solution)/shard_map/ppermute | solution.py:45
  155.1 3.4 %copy-done.1 = bf16[1024,4096]{1,0:T(8,128)(2,1)S(1)} copy-done((bf16[1024,4096]{1,0:T(8,128)(2,1)S(1)}, bf16[1024,4096]{1,0:T(8,128)(2,1)}, u32[]{:S(2)}) %copy-start.1) | copy-done | bytes 8388632
  158.4 1.0 copy-done.6
  159.5 5.2 %slope_rows.1 = (f32[1,1152]{1,0:T(1,128)S(1)}, f32[1,1152]{1,0:T(1,128)S(1)}, f32[1,1152]{1,0:T(1,128)S(1)}, f32[1,1152]{1,0:T(1,128)S(1)}) custom-call(s32[1]{0:T(128)} %bitcast.8.z_ref, bf16[1024,4096]{1,0:T(8,128)(2,1)S(1)} %copy-done.1, f32[1024,1]{1,0:T(8,128)S(1)} %copy-done.6, f32[1,128]{1,0:T(1,128)S(1)} %get-tuple-element.47.loss_ref, ...), custom_call_target="tpu_custom_call" | custom-call | flops 16777216 | bytes 8388608 | tf_op jit(solution)/shard_map/slope_rows/pallas_call | solution.py:256
  164.8 5.4 %collective-permute-done.21 = f32[1,1152]{1,0:T(1,128)S(1)} collective-permute-done((f32[1,1152]{1,0:T(1,128)S(1)}, f32[1,1152]{1,0:T(1,128)S(1)}, u32[]{:S(2)}, u32[]{:S(2)}) %collective-permute-start.21) | collective-permute-done | bytes 4640 | tf_op jit(solution)/shard_map/ppermute | solution.py:45
  170.2 4.5 %collective-permute-done.22 = f32[1,1152]{1,0:T(1,128)S(1)} collective-permute-done((f32[1,1152]{1,0:T(1,128)S(1)}, f32[1,1152]{1,0:T(1,128)S(1)}, u32[]{:S(2)}, u32[]{:S(2)}) %collective-permute-start.22) | collective-permute-done | bytes 4640 | tf_op jit(solution)/shard_map/ppermute | solution.py:45
  174.7 3.6 %collective-permute-done.23 = f32[1,1152]{1,0:T(1,128)S(1)} collective-permute-done((f32[1,1152]{1,0:T(1,128)S(1)}, f32[1,1152]{1,0:T(1,128)S(1)}, u32[]{:S(2)}, u32[]{:S(2)}) %collective-permute-start.23) | collective-permute-done | bytes 4640 | tf_op jit(solution)/shard_map/ppermute | solution.py:45
  178.3 1.5 collective-permute-start.24
  180.0 2.0 collective-permute-done.24
  182.0 1.6 collective-permute-start.26
  183.8 2.9 %grad_columns.1.refs_0_ = bf16[1024,128]{1,0:T(8,128)(2,1)S(1)} custom-call(s32[32]{0:T(128)S(1)} %stack.191.order_ref, bf16[32,64,128]{2,1,0:T(8,128)(2,1)S(1)} %all-to-all-done.1.grads_ref, bf16[256,1024]{1,0:T(8,128)(2,1)S(1)} %get-tuple-element.58.refs_0_, bf16[256,1024]{1,0:T(8,128)(2,1)} %collective-permute-done.28.refs_1_, ...), custom_call_target="tpu_custom_call" | custom-call | flops 536870912 | bytes 4980864 | tf_op jit(solution)/shard_map/grad_columns/pallas_call | solution.py:31
  186.6 1.5 collective-permute-start.37
  188.7 1.5 collective-permute-start.35
  190.3 6.4 %collective-permute-done.37.refs_3_ = bf16[1024,128]{1,0:T(8,128)(2,1)S(1)} collective-permute-done((bf16[1024,128]{1,0:T(8,128)(2,1)S(1)}, bf16[1024,128]{1,0:T(8,128)(2,1)S(1)}, u32[]{:S(2)}, u32[]{:S(2)}) %collective-permute-start.37) | collective-permute-done | bytes 262176 | tf_op jit(solution)/shard_map/ppermute | solution.py:319
  196.8 4.4 %collective-permute-done.36.refs_2_ = bf16[1024,128]{1,0:T(8,128)(2,1)S(1)} collective-permute-done((bf16[1024,128]{1,0:T(8,128)(2,1)S(1)}, bf16[1024,128]{1,0:T(8,128)(2,1)S(1)}, u32[]{:S(2)}, u32[]{:S(2)}) %collective-permute-start.36) | collective-permute-done | bytes 262176 | tf_op jit(solution)/shard_map/ppermute | solution.py:319
  202.5 1.9 collective-permute-start.44
  204.4 1.8 collective-permute-done.44
  206.5 4.2 %collective-permute-done.43 = f32[1,1024]{1,0:T(1,128)S(1)} collective-permute-done((f32[1,1024]{1,0:T(1,128)S(1)}, f32[1,1024]{1,0:T(1,128)S(1)}, u32[]{:S(2)}, u32[]{:S(2)}) %collective-permute-start.43) | collective-permute-done | bytes 4128 | tf_op jit(solution)/shard_map/ppermute | solution.py:45
  210.7 1.2 collective-permute-start.42
  213.4 2.7 %collective-permute-done.42 = f32[1,1024]{1,0:T(1,128)S(1)} collective-permute-done((f32[1,1024]{1,0:T(1,128)S(1)}, f32[1,1024]{1,0:T(1,128)S(1)}, u32[]{:S(2)}, u32[]{:S(2)}) %collective-permute-start.42) | collective-permute-done | bytes 4128 | tf_op jit(solution)/shard_map/ppermute | solution.py:45
  216.7 4.3 %finish.1 = f32[1024,1024]{1,0:T(8,128)} custom-call(s32[8]{0:T(128)S(1)} %stack.152.place_ref, f32[1024,1]{1,0:T(8,128)S(1)} %copy.17.slope_ref, f32[1,1024]{1,0:T(1,128)S(1)} %bitcast.73, bf16[1024,128]{1,0:T(8,128)(2,1)S(1)} %grad_columns.1.refs_0_, bf16[1024,128]{1,0:T(8,128)(2,1)} %collective-permute-done.35.refs_1_, ...), custom_call_target="tpu_custom_call" | custom-call | bytes 6299680 | tf_op jit(solution)/shard_map/finish/pallas_call | solution.py:31
  (108 shorter events, 13.3 us)
Async XLA Ops:
  0.6 8.2 %copy-start = (s32[64,32]{0,1:T(8,128)S(1)}, s32[64,32]{0,1:T(8,128)}, u32[]{:S(2)}) copy-start(s32[64,32]{0,1:T(8,128)} %param.10) | copy-start | bytes 24580
  2.7 27.5 %collective-permute-start.2 = (f32[1,1024]{1,0:T(1,128)S(1)}, f32[1,1024]{1,0:T(1,128)S(1)}, u32[]{:S(2)}, u32[]{:S(2)}) collective-permute-start(f32[1,1024]{1,0:T(1,128)S(1)} %bitcast.79), channel_id=1, source_target_pairs={{0,12},{4,0},{8,4},{12,8},{1,13},{5,1},{9,5},{13,9},{2,14},{6,2},{... | collective-permute-start | bytes 12296 | tf_op jit(solution)/shard_map/ppermute | solution.py:45
  7.8 22.3 %collective-permute-start.1 = (f32[1,1024]{1,0:T(1,128)S(1)}, f32[1,1024]{1,0:T(1,128)S(1)}, u32[]{:S(2)}, u32[]{:S(2)}) collective-permute-start(f32[1,1024]{1,0:T(1,128)S(1)} %bitcast.80), channel_id=1, source_target_pairs={{0,8},{4,12},{8,0},{12,4},{1,9},{5,13},{9,1},{13,5},{2,10},{6,14},... | collective-permute-start | bytes 12296 | tf_op jit(solution)/shard_map/ppermute | solution.py:45
  7.8 22.3 %collective-permute-start = (f32[1,1024]{1,0:T(1,128)S(1)}, f32[1,1024]{1,0:T(1,128)S(1)}, u32[]{:S(2)}, u32[]{:S(2)}) collective-permute-start(f32[1,1024]{1,0:T(1,128)S(1)} %bitcast.81), channel_id=1, source_target_pairs={{0,4},{4,8},{8,12},{12,0},{1,5},{5,9},{9,13},{13,1},{2,6},{6,10},{... | collective-permute-start | bytes 12296 | tf_op jit(solution)/shard_map/ppermute | solution.py:45
  9.5 51.3 %all-to-all-start = ((s32[4,1,512]{2,1,0:T(1,128)}), s32[4,1,512]{2,1,0:T(1,128)}, u32[]{:S(2)}, u32[]{:S(2)}) async-start(s32[4,1,512]{2,1,0:T(1,128)} %reshape.87), calls=%async_computation | async-start | bytes 16384 | tf_op jit(solution)/shard_map/all_to_all | solution.py:349
  19.3 10.5 %copy-start.16 = (s32[64]{0:T(128)S(1)}, s32[64]{0:T(128)}, u32[]{:S(2)}) copy-start(s32[64]{0:T(128)} %param.11) | copy-start | bytes 772
  30.2 14.6 %copy-start.3 = (bf16[1024,1024]{1,0:T(8,128)(2,1)S(1)}, bf16[1024,1024]{1,0:T(8,128)(2,1)}, u32[]{:S(2)}) copy-start(bf16[1024,1024]{1,0:T(8,128)(2,1)} %refs_4_.5) | copy-start | bytes 6291460
  30.2 23.1 %copy-start.2 = (bf16[1024,1024]{1,0:T(8,128)(2,1)S(1)}, bf16[1024,1024]{1,0:T(8,128)(2,1)}, u32[]{:S(2)}) copy-start(bf16[1024,1024]{1,0:T(8,128)(2,1)} %refs_4_.7) | copy-start | bytes 6291460
  40.0 13.3 %copy-start.5 = (f32[1024,1]{1,0:T(8,128)}, f32[1024,1]{1,0:T(8,128)S(1)}, u32[]{:S(2)}) copy-start(f32[1024,1]{1,0:T(8,128)S(1)} %get-tuple-element.31.curve_ref) | copy-start | bytes 12292
  40.0 8.2 %collective-permute-start.3 = (bf16[64,1024]{1,0:T(8,128)(2,1)S(1)}, bf16[64,1024]{1,0:T(8,128)(2,1)S(1)}, u32[]{:S(2)}, u32[]{:S(2)}) collective-permute-start(bf16[64,1024]{1,0:T(8,128)(2,1)S(1)} %get-tuple-element.33), channel_id=1, source_target_pairs={{0,4},{4,8},{8,12},{12,0},{1,5},{5,9},{9,13},{13,1},{2,6},{6,10},{... | collective-permute-start | bytes 393224 | tf_op jit(solution)/shard_map/ppermute | solution.py:45
  42.5 10.9 %collective-permute-start.4 = (bf16[64,1024]{1,0:T(8,128)(2,1)S(1)}, bf16[64,1024]{1,0:T(8,128)(2,1)S(1)}, u32[]{:S(2)}, u32[]{:S(2)}) collective-permute-start(bf16[64,1024]{1,0:T(8,128)(2,1)S(1)} %get-tuple-element.34), channel_id=1, source_target_pairs={{0,8},{4,12},{8,0},{12,4},{1,9},{5,13},{9,1},{13,5},{2,10},{6,14},... | collective-permute-start | bytes 393224 | tf_op jit(solution)/shard_map/ppermute | solution.py:45
  43.4 10.0 %collective-permute-start.5 = (bf16[64,1024]{1,0:T(8,128)(2,1)S(1)}, bf16[64,1024]{1,0:T(8,128)(2,1)S(1)}, u32[]{:S(2)}, u32[]{:S(2)}) collective-permute-start(bf16[64,1024]{1,0:T(8,128)(2,1)S(1)} %get-tuple-element.35), channel_id=1, source_target_pairs={{0,12},{4,0},{8,4},{12,8},{1,13},{5,1},{9,5},{13,9},{2,14},{6,2},{... | collective-permute-start | bytes 393224 | tf_op jit(solution)/shard_map/ppermute | solution.py:45
  53.4 55.4 %copy-start.8 = (bf16[64,1024]{1,0:T(8,128)(2,1)S(1)}, bf16[64,1024]{1,0:T(8,128)(2,1)}, u32[]{:S(2)}) copy-start(bf16[64,1024]{1,0:T(8,128)(2,1)} %refs_4_.6) | copy-start | bytes 393220
  54.8 9.9 %collective-permute-start.6 = (bf16[64,1024]{1,0:T(8,128)(2,1)}, bf16[64,1024]{1,0:T(8,128)(2,1)S(1)}, u32[]{:S(2)}, u32[]{:S(2)}) collective-permute-start(bf16[64,1024]{1,0:T(8,128)(2,1)} %get-tuple-element.37), channel_id=1, source_target_pairs={{0,12},{4,0},{8,4},{12,8},{1,13},{5,1},{9,5},{13,9},{2,14},{6,2},{... | collective-permute-start | bytes 393224 | tf_op jit(solution)/shard_map/ppermute | solution.py:45
  58.8 12.8 %collective-permute-start.7 = (bf16[64,1024]{1,0:T(8,128)(2,1)}, bf16[64,1024]{1,0:T(8,128)(2,1)S(1)}, u32[]{:S(2)}, u32[]{:S(2)}) collective-permute-start(bf16[64,1024]{1,0:T(8,128)(2,1)} %get-tuple-element.38), channel_id=1, source_target_pairs={{0,8},{4,12},{8,0},{12,4},{1,9},{5,13},{9,1},{13,5},{2,10},{6,14},... | collective-permute-start | bytes 393224 | tf_op jit(solution)/shard_map/ppermute | solution.py:45
  59.5 12.1 %collective-permute-start.8 = (bf16[64,1024]{1,0:T(8,128)(2,1)S(1)}, bf16[64,1024]{1,0:T(8,128)(2,1)S(1)}, u32[]{:S(2)}, u32[]{:S(2)}) collective-permute-start(bf16[64,1024]{1,0:T(8,128)(2,1)S(1)} %get-tuple-element.39), channel_id=1, source_target_pairs={{0,4},{4,8},{8,12},{12,0},{1,5},{5,9},{9,13},{13,1},{2,6},{6,10},{... | collective-permute-start | bytes 393224 | tf_op jit(solution)/shard_map/ppermute | solution.py:45
  71.6 0.6 copy-start.9
  72.2 0.9 copy-start.10
  73.9 0.6 copy-start.11
  74.5 34.2 %copy-start.12 = (f32[64,1]{1,0:T(8,128)S(1)}, f32[64,1]{1,0:T(8,128)}, u32[]{:S(2)}) copy-start(f32[64,1]{1,0:T(8,128)} %copy-done.11) | copy-start | bytes 772
  74.5 5.0 %collective-permute-start.11 = (bf16[64,1024]{1,0:T(8,128)(2,1)}, bf16[64,1024]{1,0:T(8,128)(2,1)S(1)}, u32[]{:S(2)}, u32[]{:S(2)}) collective-permute-start(bf16[64,1024]{1,0:T(8,128)(2,1)} %get-tuple-element.40.refs_0_.refs_7_), channel_id=1, source_target_pairs={{0,3},{1,0},{2,1},{3,2},{4,7},{5,4},{6,5},{7,6},{8,11},{9,8},{10,9... | collective-permute-start | bytes 393224 | tf_op jit(solution)/shard_map/ppermute | solution.py:45
  75.0 8.5 %collective-permute-start.10 = (bf16[64,1024]{1,0:T(8,128)(2,1)}, bf16[64,1024]{1,0:T(8,128)(2,1)S(1)}, u32[]{:S(2)}, u32[]{:S(2)}) collective-permute-start(bf16[64,1024]{1,0:T(8,128)(2,1)} %get-tuple-element.40.refs_0_.refs_7_), channel_id=1, source_target_pairs={{0,2},{1,3},{2,0},{3,1},{4,6},{5,7},{6,4},{7,5},{8,10},{9,11},{10,... | collective-permute-start | bytes 393224 | tf_op jit(solution)/shard_map/ppermute | solution.py:45
  76.2 7.3 %collective-permute-start.9 = (bf16[64,1024]{1,0:T(8,128)(2,1)}, bf16[64,1024]{1,0:T(8,128)(2,1)}, u32[]{:S(2)}, u32[]{:S(2)}) collective-permute-start(bf16[64,1024]{1,0:T(8,128)(2,1)} %get-tuple-element.40.refs_0_.refs_7_), channel_id=1, source_target_pairs={{0,1},{1,2},{2,3},{3,0},{4,5},{5,6},{6,7},{7,4},{8,9},{9,10},{10,1... | collective-permute-start | bytes 393224 | tf_op jit(solution)/shard_map/ppermute | solution.py:45
  77.2 0.7 copy-start.15
  83.5 1.6 copy-start.4
  85.1 0.7 copy-start.14
  88.1 3.9 %collective-permute-start.12 = (bf16[64,1152]{1,0:T(8,128)(2,1)S(1)}, bf16[64,1152]{1,0:T(8,128)(2,1)S(1)}, u32[]{:S(2)}, u32[]{:S(2)}) collective-permute-start(bf16[64,1152]{1,0:T(8,128)(2,1)S(1)} %get-tuple-element.42), channel_id=1, source_target_pairs={{0,3},{1,0},{2,1},{3,2},{4,7},{5,4},{6,5},{7,6},{8,11},{9,8},{10,9... | collective-permute-start | bytes 442376 | tf_op jit(solution)/shard_map/ppermute | solution.py:45
  88.1 19.5 %collective-permute-start.13 = (bf16[64,1152]{1,0:T(8,128)(2,1)S(1)}, bf16[64,1152]{1,0:T(8,128)(2,1)S(1)}, u32[]{:S(2)}, u32[]{:S(2)}) collective-permute-start(bf16[64,1152]{1,0:T(8,128)(2,1)S(1)} %get-tuple-element.43), channel_id=1, source_target_pairs={{0,2},{1,3},{2,0},{3,1},{4,6},{5,7},{6,4},{7,5},{8,10},{9,11},{10,... | collective-permute-start | bytes 442376 | tf_op jit(solution)/shard_map/ppermute | solution.py:45
  89.2 19.6 %collective-permute-start.14 = (bf16[64,1152]{1,0:T(8,128)(2,1)S(1)}, bf16[64,1152]{1,0:T(8,128)(2,1)S(1)}, u32[]{:S(2)}, u32[]{:S(2)}) collective-permute-start(bf16[64,1152]{1,0:T(8,128)(2,1)S(1)} %get-tuple-element.44), channel_id=1, source_target_pairs={{0,1},{1,2},{2,3},{3,0},{4,5},{5,6},{6,7},{7,4},{8,9},{9,10},{10,1... | collective-permute-start | bytes 442376 | tf_op jit(solution)/shard_map/ppermute | solution.py:45
  89.3 55.9 %collective-permute-start.30 = (bf16[256,1024]{1,0:T(8,128)(2,1)S(1)}, bf16[256,1024]{1,0:T(8,128)(2,1)}, u32[]{:S(2)}, u32[]{:S(2)}) collective-permute-start(bf16[256,1024]{1,0:T(8,128)(2,1)S(1)} %get-tuple-element.58.refs_0_), channel_id=1, source_target_pairs={{0,18},{1,19},{2,16},{3,17},{16,2},{17,3},{18,0},{19,1},{4,22},{5,... | collective-permute-start | bytes 1572872 | tf_op jit(solution)/shard_map/ppermute | solution.py:319
  91.3 53.9 %collective-permute-start.29 = (bf16[256,1024]{1,0:T(8,128)(2,1)S(1)}, bf16[256,1024]{1,0:T(8,128)(2,1)}, u32[]{:S(2)}, u32[]{:S(2)}) collective-permute-start(bf16[256,1024]{1,0:T(8,128)(2,1)S(1)} %get-tuple-element.58.refs_0_), channel_id=1, source_target_pairs={{0,16},{1,17},{2,18},{3,19},{16,0},{17,1},{18,2},{19,3},{4,20},{5,... | collective-permute-start | bytes 1572872 | tf_op jit(solution)/shard_map/ppermute | solution.py:319
  91.9 53.4 %collective-permute-start.28 = (bf16[256,1024]{1,0:T(8,128)(2,1)S(1)}, bf16[256,1024]{1,0:T(8,128)(2,1)}, u32[]{:S(2)}, u32[]{:S(2)}) collective-permute-start(bf16[256,1024]{1,0:T(8,128)(2,1)S(1)} %get-tuple-element.58.refs_0_), channel_id=1, source_target_pairs={{0,2},{1,3},{2,0},{3,1},{16,18},{17,19},{18,16},{19,17},{4,6},{5,7... | collective-permute-start | bytes 1572872 | tf_op jit(solution)/shard_map/ppermute | solution.py:319
  110.1 0.8 copy-start.7
  110.9 72.8 %all-to-all-start.1 = ((bf16[32,64,128]{2,1,0:T(8,128)(2,1)}), bf16[32,64,128]{2,1,0:T(8,128)(2,1)S(1)}, u32[]{:S(2)}, u32[]{:S(2)}) async-start(bf16[32,64,128]{2,1,0:T(8,128)(2,1)} %copy-done.7), calls=%async_computation.1 | async-start | bytes 1048576 | tf_op jit(solution)/shard_map/all_to_all | solution.py:391
  113.6 12.9 %collective-permute-start.17 = (bf16[64,1024]{1,0:T(8,128)(2,1)S(1)}, bf16[64,1024]{1,0:T(8,128)(2,1)S(1)}, u32[]{:S(2)}, u32[]{:S(2)}) collective-permute-start(bf16[64,1024]{1,0:T(8,128)(2,1)S(1)} %get-tuple-element.48.refs_0_), channel_id=1, source_target_pairs={{0,12},{4,0},{8,4},{12,8},{1,13},{5,1},{9,5},{13,9},{2,14},{6,2},{... | collective-permute-start | bytes 393224 | tf_op jit(solution)/shard_map/ppermute | solution.py:45
  117.2 22.6 %collective-permute-start.16 = (bf16[64,1024]{1,0:T(8,128)(2,1)S(1)}, bf16[64,1024]{1,0:T(8,128)(2,1)S(1)}, u32[]{:S(2)}, u32[]{:S(2)}) collective-permute-start(bf16[64,1024]{1,0:T(8,128)(2,1)S(1)} %get-tuple-element.48.refs_0_), channel_id=1, source_target_pairs={{0,8},{4,12},{8,0},{12,4},{1,9},{5,13},{9,1},{13,5},{2,10},{6,14},... | collective-permute-start | bytes 393224 | tf_op jit(solution)/shard_map/ppermute | solution.py:45
  126.5 14.0 %collective-permute-start.15 = (bf16[64,1024]{1,0:T(8,128)(2,1)S(1)}, bf16[64,1024]{1,0:T(8,128)(2,1)S(1)}, u32[]{:S(2)}, u32[]{:S(2)}) collective-permute-start(bf16[64,1024]{1,0:T(8,128)(2,1)S(1)} %get-tuple-element.48.refs_0_), channel_id=1, source_target_pairs={{0,4},{4,8},{8,12},{12,0},{1,5},{5,9},{9,13},{13,1},{2,6},{6,10},{... | collective-permute-start | bytes 393224 | tf_op jit(solution)/shard_map/ppermute | solution.py:45
  141.3 5.5 %collective-permute-start.18 = (bf16[64,1024]{1,0:T(8,128)(2,1)S(1)}, bf16[64,1024]{1,0:T(8,128)(2,1)S(1)}, u32[]{:S(2)}, u32[]{:S(2)}) collective-permute-start(bf16[64,1024]{1,0:T(8,128)(2,1)S(1)} %get-tuple-element.50), channel_id=1, source_target_pairs={{0,12},{4,0},{8,4},{12,8},{1,13},{5,1},{9,5},{13,9},{2,14},{6,2},{... | collective-permute-start | bytes 393224 | tf_op jit(solution)/shard_map/ppermute | solution.py:45
  142.2 12.9 %collective-permute-start.19 = (bf16[64,1024]{1,0:T(8,128)(2,1)S(1)}, bf16[64,1024]{1,0:T(8,128)(2,1)S(1)}, u32[]{:S(2)}, u32[]{:S(2)}) collective-permute-start(bf16[64,1024]{1,0:T(8,128)(2,1)S(1)} %get-tuple-element.51), channel_id=1, source_target_pairs={{0,8},{4,12},{8,0},{12,4},{1,9},{5,13},{9,1},{13,5},{2,10},{6,14},... | collective-permute-start | bytes 393224 | tf_op jit(solution)/shard_map/ppermute | solution.py:45
  145.2 9.8 %collective-permute-start.20 = (bf16[64,1024]{1,0:T(8,128)(2,1)S(1)}, bf16[64,1024]{1,0:T(8,128)(2,1)S(1)}, u32[]{:S(2)}, u32[]{:S(2)}) collective-permute-start(bf16[64,1024]{1,0:T(8,128)(2,1)S(1)} %get-tuple-element.52), channel_id=1, source_target_pairs={{0,4},{4,8},{8,12},{12,0},{1,5},{5,9},{9,13},{13,1},{2,6},{6,10},{... | collective-permute-start | bytes 393224 | tf_op jit(solution)/shard_map/ppermute | solution.py:45
  145.2 36.8 %collective-permute-start.31 = (bf16[256,1024]{1,0:T(8,128)(2,1)S(1)}, bf16[256,1024]{1,0:T(8,128)(2,1)}, u32[]{:S(2)}, u32[]{:S(2)}) collective-permute-start(bf16[256,1024]{1,0:T(8,128)(2,1)S(1)} %get-tuple-element.58.refs_0_), channel_id=1, source_target_pairs={{0,1},{1,0},{2,3},{3,2},{16,17},{17,16},{18,19},{19,18},{4,5},{5,4... | collective-permute-start | bytes 1572872 | tf_op jit(solution)/shard_map/ppermute | solution.py:319
  145.3 38.3 %collective-permute-start.34 = (bf16[256,1024]{1,0:T(8,128)(2,1)}, bf16[256,1024]{1,0:T(8,128)(2,1)}, u32[]{:S(2)}, u32[]{:S(2)}) collective-permute-start(bf16[256,1024]{1,0:T(8,128)(2,1)} %collective-permute-done.30.refs_3_), channel_id=1, source_target_pairs={{0,1},{1,0},{2,3},{3,2},{16,17},{17,16},{18,19},{19,18},{4,5},{5,4... | collective-permute-start | bytes 1572872 | tf_op jit(solution)/shard_map/ppermute | solution.py:319
  146.7 37.0 %collective-permute-start.33 = (bf16[256,1024]{1,0:T(8,128)(2,1)}, bf16[256,1024]{1,0:T(8,128)(2,1)}, u32[]{:S(2)}, u32[]{:S(2)}) collective-permute-start(bf16[256,1024]{1,0:T(8,128)(2,1)} %collective-permute-done.29.refs_2_), channel_id=1, source_target_pairs={{0,1},{1,0},{2,3},{3,2},{16,17},{17,16},{18,19},{19,18},{4,5},{5,4... | collective-permute-start | bytes 1572872 | tf_op jit(solution)/shard_map/ppermute | solution.py:319
  155.1 28.7 %collective-permute-start.32 = (bf16[256,1024]{1,0:T(8,128)(2,1)}, bf16[256,1024]{1,0:T(8,128)(2,1)}, u32[]{:S(2)}, u32[]{:S(2)}) collective-permute-start(bf16[256,1024]{1,0:T(8,128)(2,1)} %collective-permute-done.28.refs_1_), channel_id=1, source_target_pairs={{0,1},{1,0},{2,3},{3,2},{16,17},{17,16},{18,19},{19,18},{4,5},{5,4... | collective-permute-start | bytes 1572872 | tf_op jit(solution)/shard_map/ppermute | solution.py:319
  155.1 3.4 %copy-start.1 = (bf16[1024,4096]{1,0:T(8,128)(2,1)S(1)}, bf16[1024,4096]{1,0:T(8,128)(2,1)}, u32[]{:S(2)}) copy-start(bf16[1024,4096]{1,0:T(8,128)(2,1)} %fusion.1.normed_ref) | copy-start | bytes 25165828
  158.4 1.0 copy-start.6
  164.7 52.0 %copy-start.13 = (f32[1024]{0:T(1024)S(1)}, f32[1024]{0:T(1024)}, u32[]{:S(2)}) copy-start(f32[1024]{0:T(1024)} %param.14) | copy-start | bytes 12292
  164.7 5.5 %collective-permute-start.21 = (f32[1,1152]{1,0:T(1,128)S(1)}, f32[1,1152]{1,0:T(1,128)S(1)}, u32[]{:S(2)}, u32[]{:S(2)}) collective-permute-start(f32[1,1152]{1,0:T(1,128)S(1)} %get-tuple-element.54), channel_id=1, source_target_pairs={{0,4},{4,8},{8,12},{12,0},{1,5},{5,9},{9,13},{13,1},{2,6},{6,10},{... | collective-permute-start | bytes 13832 | tf_op jit(solution)/shard_map/ppermute | solution.py:45
  170.2 4.5 %collective-permute-start.22 = (f32[1,1152]{1,0:T(1,128)S(1)}, f32[1,1152]{1,0:T(1,128)S(1)}, u32[]{:S(2)}, u32[]{:S(2)}) collective-permute-start(f32[1,1152]{1,0:T(1,128)S(1)} %get-tuple-element.55), channel_id=1, source_target_pairs={{0,8},{4,12},{8,0},{12,4},{1,9},{5,13},{9,1},{13,5},{2,10},{6,14},... | collective-permute-start | bytes 13832 | tf_op jit(solution)/shard_map/ppermute | solution.py:45
  174.7 3.6 %collective-permute-start.23 = (f32[1,1152]{1,0:T(1,128)S(1)}, f32[1,1152]{1,0:T(1,128)S(1)}, u32[]{:S(2)}, u32[]{:S(2)}) collective-permute-start(f32[1,1152]{1,0:T(1,128)S(1)} %get-tuple-element.56), channel_id=1, source_target_pairs={{0,12},{4,0},{8,4},{12,8},{1,13},{5,1},{9,5},{13,9},{2,14},{6,2},{... | collective-permute-start | bytes 13832 | tf_op jit(solution)/shard_map/ppermute | solution.py:45
  178.3 3.7 %collective-permute-start.24 = (f32[1,1152]{1,0:T(1,128)S(1)}, f32[1,1152]{1,0:T(1,128)S(1)}, u32[]{:S(2)}, u32[]{:S(2)}) collective-permute-start(f32[1,1152]{1,0:T(1,128)S(1)} %add_add_fusion.1), channel_id=1, source_target_pairs={{0,16},{16,0},{1,17},{17,1},{2,18},{18,2},{3,19},{19,3},{4,20},{20... | collective-permute-start | bytes 13832 | tf_op jit(solution)/shard_map/ppermute | solution.py:45
  182.0 6.7 %collective-permute-start.27 = (f32[1,1152]{1,0:T(1,128)S(1)}, f32[1,1152]{1,0:T(1,128)S(1)}, u32[]{:S(2)}, u32[]{:S(2)}) collective-permute-start(f32[1,1152]{1,0:T(1,128)S(1)} %add.441), channel_id=1, source_target_pairs={{0,3},{1,0},{2,1},{3,2},{4,7},{5,4},{6,5},{7,6},{8,11},{9,8},{10,9... | collective-permute-start | bytes 13832 | tf_op jit(solution)/shard_map/ppermute | solution.py:45
  182.0 8.2 %collective-permute-start.26 = (f32[1,1152]{1,0:T(1,128)S(1)}, f32[1,1152]{1,0:T(1,128)S(1)}, u32[]{:S(2)}, u32[]{:S(2)}) collective-permute-start(f32[1,1152]{1,0:T(1,128)S(1)} %add.441), channel_id=1, source_target_pairs={{0,2},{1,3},{2,0},{3,1},{4,6},{5,7},{6,4},{7,5},{8,10},{9,11},{10,... | collective-permute-start | bytes 13832 | tf_op jit(solution)/shard_map/ppermute | solution.py:45
  183.6 6.6 %collective-permute-start.25 = (f32[1,1152]{1,0:T(1,128)S(1)}, f32[1,1152]{1,0:T(1,128)S(1)}, u32[]{:S(2)}, u32[]{:S(2)}) collective-permute-start(f32[1,1152]{1,0:T(1,128)S(1)} %add.441), channel_id=1, source_target_pairs={{0,1},{1,2},{2,3},{3,0},{4,5},{5,6},{6,7},{7,4},{8,9},{9,10},{10,1... | collective-permute-start | bytes 13832 | tf_op jit(solution)/shard_map/ppermute | solution.py:45
  186.6 10.1 %collective-permute-start.37 = (bf16[1024,128]{1,0:T(8,128)(2,1)S(1)}, bf16[1024,128]{1,0:T(8,128)(2,1)S(1)}, u32[]{:S(2)}, u32[]{:S(2)}) collective-permute-start(bf16[1024,128]{1,0:T(8,128)(2,1)S(1)} %grad_columns.1.refs_0_), channel_id=1, source_target_pairs={{0,18},{1,19},{2,16},{3,17},{16,2},{17,3},{18,0},{19,1},{4,22},{5,... | collective-permute-start | bytes 786440 | tf_op jit(solution)/shard_map/ppermute | solution.py:319
  188.1 13.0 %collective-permute-start.36 = (bf16[1024,128]{1,0:T(8,128)(2,1)S(1)}, bf16[1024,128]{1,0:T(8,128)(2,1)S(1)}, u32[]{:S(2)}, u32[]{:S(2)}) collective-permute-start(bf16[1024,128]{1,0:T(8,128)(2,1)S(1)} %grad_columns.1.refs_0_), channel_id=1, source_target_pairs={{0,16},{1,17},{2,18},{3,19},{16,0},{17,1},{18,2},{19,3},{4,20},{5,... | collective-permute-start | bytes 786440 | tf_op jit(solution)/shard_map/ppermute | solution.py:319
  188.7 13.3 %collective-permute-start.35 = (bf16[1024,128]{1,0:T(8,128)(2,1)S(1)}, bf16[1024,128]{1,0:T(8,128)(2,1)}, u32[]{:S(2)}, u32[]{:S(2)}) collective-permute-start(bf16[1024,128]{1,0:T(8,128)(2,1)S(1)} %grad_columns.1.refs_0_), channel_id=1, source_target_pairs={{0,2},{1,3},{2,0},{3,1},{16,18},{17,19},{18,16},{19,17},{4,6},{5,7... | collective-permute-start | bytes 786440 | tf_op jit(solution)/shard_map/ppermute | solution.py:319
  190.3 26.5 %collective-permute-start.38 = (bf16[1024,128]{1,0:T(8,128)(2,1)S(1)}, bf16[1024,128]{1,0:T(8,128)(2,1)}, u32[]{:S(2)}, u32[]{:S(2)}) collective-permute-start(bf16[1024,128]{1,0:T(8,128)(2,1)S(1)} %grad_columns.1.refs_0_), channel_id=1, source_target_pairs={{0,1},{1,0},{2,3},{3,2},{16,17},{17,16},{18,19},{19,18},{4,5},{5,4... | collective-permute-start | bytes 786440 | tf_op jit(solution)/shard_map/ppermute | solution.py:319
  196.8 20.0 %collective-permute-start.41 = (bf16[1024,128]{1,0:T(8,128)(2,1)S(1)}, bf16[1024,128]{1,0:T(8,128)(2,1)}, u32[]{:S(2)}, u32[]{:S(2)}) collective-permute-start(bf16[1024,128]{1,0:T(8,128)(2,1)S(1)} %collective-permute-done.37.refs_3_), channel_id=1, source_target_pairs={{0,1},{1,0},{2,3},{3,2},{16,17},{17,16},{18,19},{19,18},{4,5},{5,4... | collective-permute-start | bytes 786440 | tf_op jit(solution)/shard_map/ppermute | solution.py:319
  201.1 15.6 %collective-permute-start.40 = (bf16[1024,128]{1,0:T(8,128)(2,1)S(1)}, bf16[1024,128]{1,0:T(8,128)(2,1)}, u32[]{:S(2)}, u32[]{:S(2)}) collective-permute-start(bf16[1024,128]{1,0:T(8,128)(2,1)S(1)} %collective-permute-done.36.refs_2_), channel_id=1, source_target_pairs={{0,1},{1,0},{2,3},{3,2},{16,17},{17,16},{18,19},{19,18},{4,5},{5,4... | collective-permute-start | bytes 786440 | tf_op jit(solution)/shard_map/ppermute | solution.py:319
  202.0 14.7 %collective-permute-start.39 = (bf16[1024,128]{1,0:T(8,128)(2,1)}, bf16[1024,128]{1,0:T(8,128)(2,1)}, u32[]{:S(2)}, u32[]{:S(2)}) collective-permute-start(bf16[1024,128]{1,0:T(8,128)(2,1)} %collective-permute-done.35.refs_1_), channel_id=1, source_target_pairs={{0,1},{1,0},{2,3},{3,2},{16,17},{17,16},{18,19},{19,18},{4,5},{5,4... | collective-permute-start | bytes 786440 | tf_op jit(solution)/shard_map/ppermute | solution.py:319
  202.5 3.7 %collective-permute-start.44 = (f32[1,1024]{1,0:T(1,128)S(1)}, f32[1,1024]{1,0:T(1,128)S(1)}, u32[]{:S(2)}, u32[]{:S(2)}) collective-permute-start(f32[1,1024]{1,0:T(1,128)S(1)} %bitcast.75), channel_id=1, source_target_pairs={{0,12},{4,0},{8,4},{12,8},{1,13},{5,1},{9,5},{13,9},{2,14},{6,2},{... | collective-permute-start | bytes 12296 | tf_op jit(solution)/shard_map/ppermute | solution.py:45
  206.2 4.5 %collective-permute-start.43 = (f32[1,1024]{1,0:T(1,128)S(1)}, f32[1,1024]{1,0:T(1,128)S(1)}, u32[]{:S(2)}, u32[]{:S(2)}) collective-permute-start(f32[1,1024]{1,0:T(1,128)S(1)} %bitcast.76), channel_id=1, source_target_pairs={{0,8},{4,12},{8,0},{12,4},{1,9},{5,13},{9,1},{13,5},{2,10},{6,14},... | collective-permute-start | bytes 12296 | tf_op jit(solution)/shard_map/ppermute | solution.py:45
  210.7 5.4 %collective-permute-start.42 = (f32[1,1024]{1,0:T(1,128)S(1)}, f32[1,1024]{1,0:T(1,128)S(1)}, u32[]{:S(2)}, u32[]{:S(2)}) collective-permute-start(f32[1,1024]{1,0:T(1,128)S(1)} %bitcast.77), channel_id=1, source_target_pairs={{0,4},{4,8},{8,12},{12,0},{1,5},{5,9},{9,13},{13,1},{2,6},{6,10},{... | collective-permute-start | bytes 12296 | tf_op jit(solution)/shard_map/ppermute | solution.py:45
